TPU v7x, 512 devices: a whole 4x4x16 slice. The times are simulated.
512 devices in a mesh: tile: 32 (over x, z_lo), beam: 16 (over y, z_hi, core).
Axes of the slice: x: 4, y: 4, z: 16 (z_hi: 2, z_lo: 8; z = z_hi * 8 + z_lo), core: 2. Of those that a mesh axis runs over, the one named last changes fastest.
Arguments:
- smatrix: bfloat16 [2, 2048, 512, 512], P(None, ('beam', 'tile')), may hold values from -6 to 6
- offset_y: int32 [512], replicated, may hold values from 0 to 511, as said below
- offset_x: int32 [512], replicated, may hold values from 0 to 511
- beam_qx: int32 [2048], P('beam'), may hold values from -64 to 63
- beam_qy: int32 [2048], P('beam'), may hold values from -64 to 63
- beam_amp: float32 [2048], P('beam'), may hold values from 0.5 to 2
- beam_phase: float32 [2048], P('beam'), may hold values from -3.140625 to 3.140625
Outputs:
- intensity: float32 [512, 128, 128], P(('tile', 'beam'))
Inputs may be any that keep to these rules, and one draw needn't show every extreme that they name: `offset_y`: the window of position p starts in field rows 16 * (p // 16) to 16 * (p // 16) + 15.
All inputs are finite; a program needn't handle non-finite values.
Results may differ from a plain program's by a relative error of at most 0.017.
Values may be sent and summed in bfloat16 or wider, within the bound.
A program may use at most 128 MiB of HBM per device.

v0:
```python
import math

import jax
import jax.numpy as jnp
from jax import lax
from jax.sharding import PartitionSpec as P

BEAMS = 2048
CROP = 128
POS_DEV = 16


two_pi = 2.0 * math.pi


def cut_along(shard, dim, size):
    before, after = (shard.shape[:dim], shard.shape[dim + 1 :])
    return jnp.moveaxis(shard.reshape(*before, size, -1, *after), dim, 0)


def sum_at_owner(shard, axis, dim):
    parts = cut_along(shard, dim, lax.axis_size(axis))
    arrived = lax.all_to_all(parts, axis, split_axis=0, concat_axis=0, tiled=True)
    return arrived.astype(jnp.float32).sum(axis=0)


def passed_along(value, axis, steps):
    count = lax.axis_size(axis)
    pairs = [(source, (source + steps) % count) for source in range(count)]
    return lax.ppermute(value, axis, pairs)


def cut_window(piece, begin):
    return lax.dynamic_slice_in_dim(piece, begin, CROP, 1)


def cut_columns(piece, begin):
    return lax.dynamic_slice_in_dim(piece, begin, CROP, 2)


def transform(exit_wave):
    places = jnp.arange(CROP, dtype=jnp.int32)
    ticks = places[:, None] * places[None, :] % CROP
    angle = two_pi * ticks.astype(jnp.float32) / CROP
    norm_factor = 1.0 / math.sqrt(CROP)
    table_re = jnp.cos(angle) * norm_factor
    table_im = -jnp.sin(angle) * norm_factor
    highest = lax.Precision.HIGHEST
    right_table = jnp.concatenate(
        [
            jnp.concatenate([table_re, table_im], axis=1),
            jnp.concatenate([-table_im, table_re], axis=1),
        ],
        axis=0,
    )
    left_table = jnp.concatenate(
        [
            jnp.concatenate([table_re, -table_im], axis=1),
            jnp.concatenate([table_im, table_re], axis=1),
        ],
        axis=0,
    )
    count = exit_wave.shape[0]
    joined = jnp.concatenate([exit_wave[:, 0], exit_wave[:, 1]], axis=2)
    halves = jnp.einsum("pij,jk->pik", joined, right_table, precision=highest)
    halves = (
        halves.reshape(count, CROP, 2, CROP).transpose(0, 2, 1, 3).reshape(count, 2 * CROP, CROP)
    )
    full = jnp.einsum("ui,pik->puk", left_table, halves, precision=highest)
    full_re = full[:, :CROP]
    full_im = full[:, CROP:]
    return full_re * full_re + full_im * full_im


def local(smatrix, offset_y, offset_x, beam_qx, beam_qy, beam_amp, beam_phase):
    tiles = lax.axis_size("tile")
    own_tile = lax.axis_index("tile")
    own_group = lax.axis_index("beam")
    strips = lax.all_to_all(smatrix, "tile", split_axis=2, concat_axis=1, tiled=True)
    planes, group_beams, strip, field = strips.shape
    stacked = strips.reshape(planes * group_beams, strip * field)
    reach = CROP // strip
    scale = beam_amp * (1.0 / math.sqrt(BEAMS))

    def owner_block(distance):
        owner = (own_tile - distance) % tiles
        start = owner * POS_DEV
        first_y = lax.dynamic_slice_in_dim(offset_y, start, POS_DEV)
        first_x = lax.dynamic_slice_in_dim(offset_x, start, POS_DEV)
        turns = (
            (first_x + CROP // 2)[:, None] * beam_qx[None, :]
            + (first_y + CROP // 2)[:, None] * beam_qy[None, :]
        ) % field
        angle = beam_phase[None, :] - two_pi * turns.astype(jnp.float32) / field
        w_real = (scale[None, :] * jnp.cos(angle)).astype(jnp.bfloat16)
        w_imag = (scale[None, :] * jnp.sin(angle)).astype(jnp.bfloat16)
        real_row = jnp.concatenate([w_real, -w_imag], axis=1)
        imag_row = jnp.concatenate([w_imag, w_real], axis=1)
        mixing = jnp.stack([real_row, imag_row], axis=1).reshape(2 * POS_DEV, 2 * group_beams)
        waves = jnp.dot(mixing, stacked, preferred_element_type=jnp.float32).astype(jnp.bfloat16)
        waves = waves.reshape(POS_DEV, 2, strip, field)
        extended = jnp.concatenate([waves, waves[:, :, :, :CROP]], axis=3)
        return jax.vmap(cut_columns)(extended, first_x % field)

    blocks = jnp.stack([owner_block(distance) for distance in range(reach + 1)])
    reduced = sum_at_owner(blocks.astype(jnp.float32).astype(jnp.bfloat16), "beam", 1)
    pieces = [reduced[0]]
    for distance in range(1, reach + 1):
        pieces.append(passed_along(reduced[distance], "tile", -distance))
    gathered = jnp.concatenate(pieces, axis=2)
    share = POS_DEV // lax.axis_size("beam")
    first_rows = (
        lax.dynamic_slice_in_dim(offset_y, own_tile * POS_DEV + own_group * share, share) % strip
    )
    exit_wave = jax.vmap(cut_window)(gathered, first_rows)
    return transform(exit_wave)


def solution(mesh):
    return jax.shard_map(
        local,
        mesh=mesh,
        in_specs=(
            P(None, ("beam", "tile"), None, None),
            P(),
            P(),
            P("beam"),
            P("beam"),
            P("beam"),
            P("beam"),
        ),
        out_specs=P(("tile", "beam"), None, None),
        check_vma=False,
    )
```

profile of v0, /device:TPU:1, one launch (start us, length us, event | category | flops | bytes accessed | tf_op | source)
XLA Modules:
  0.0 517.3 jit_solution(4763921726313252249)
XLA Ops:
  0.0 7.4 %copy.127 = bf16[2,4,512,512]{3,1,0,2:T(4,128)(2,1)} copy(bf16[2,4,512,512]{3,2,1,0:T(8,128)(2,1)} %param.7) | data formatting | bytes 8388608 | tf_op args[0]
  7.5 16.4 %all-to-all-start = ((bf16[2,4,512,512]{3,1,0,2:T(4,128)(2,1)}), bf16[2,4,512,512]{3,1,0,2:T(4,128)(2,1)}, u32[]{:S(2)}, u32[]{:S(2)}) async-start(bf16[2,4,512,512]{3,1,0,2:T(4,128)(2,1)} %copy.127), calls=%async_computation | async-start | bytes 8388608 | tf_op jit(solution)/shard_map/all_to_all | solution.py:79
  26.0 174.9 %all-to-all-done = bf16[2,4,512,512]{3,1,0,2:T(4,128)(2,1)} async-done(((bf16[2,4,512,512]{3,1,0,2:T(4,128)(2,1)}), bf16[2,4,512,512]{3,1,0,2:T(4,128)(2,1)}, u32[]{:S(2)}, u32[]{:S(2)}) %all-to-all-start) | async-done | bytes 4194336 | tf_op jit(solution)/shard_map/all_to_all | solution.py:79
  200.9 4.0 copy.128
  204.9 4.3 copy.177
  212.4 8.6 %copy.129 = bf16[16,2,16,640]{2,1,0,3:T(2,128)(2,1)} copy(bf16[16,2,16,640]{3,2,1,0:T(8,128)(2,1)S(1)} %pad_maximum_fusion) | data formatting | bytes 1310720 | tf_op jit(solution)/shard_map/concatenate | solution.py:102
  221.0 5.8 %gather_fusion = bf16[16,2,16,128]{2,1,3,0:T(2,128)(2,1)S(1)} fusion(bf16[16,2,16,640]{2,1,0,3:T(2,128)(2,1)} %copy.129, s32[16]{0:T(128)S(1)} %get-tuple-element.64), kind=kCustom, calls=%fused_computation | custom fusion | bytes 262400 | tf_op jit(solution)/shard_map/vmap()/gather | solution.py:38
  231.9 8.3 %copy.131 = bf16[16,2,16,640]{2,1,0,3:T(2,128)(2,1)} copy(bf16[16,2,16,640]{3,2,1,0:T(8,128)(2,1)S(1)} %pad_maximum_fusion.1) | data formatting | bytes 1310720 | tf_op jit(solution)/shard_map/concatenate | solution.py:102
  243.5 8.3 %copy.133 = bf16[16,2,16,640]{2,1,0,3:T(2,128)(2,1)} copy(bf16[16,2,16,640]{3,2,1,0:T(8,128)(2,1)S(1)} %pad_maximum_fusion.2) | data formatting | bytes 1310720 | tf_op jit(solution)/shard_map/concatenate | solution.py:102
  255.1 8.3 %copy.135 = bf16[16,2,16,640]{2,1,0,3:T(2,128)(2,1)} copy(bf16[16,2,16,640]{3,2,1,0:T(8,128)(2,1)S(1)} %pad_maximum_fusion.3) | data formatting | bytes 1310720 | tf_op jit(solution)/shard_map/concatenate | solution.py:102
  266.7 8.2 %copy.137 = bf16[16,2,16,640]{2,1,0,3:T(2,128)(2,1)} copy(bf16[16,2,16,640]{3,2,1,0:T(8,128)(2,1)S(1)} %pad_maximum_fusion.4) | data formatting | bytes 1310720 | tf_op jit(solution)/shard_map/concatenate | solution.py:102
  278.2 8.2 %copy.139 = bf16[16,2,16,640]{2,1,0,3:T(2,128)(2,1)} copy(bf16[16,2,16,640]{3,2,1,0:T(8,128)(2,1)S(1)} %pad_maximum_fusion.5) | data formatting | bytes 1310720 | tf_op jit(solution)/shard_map/concatenate | solution.py:102
  286.4 3.0 convolution_convert_fusion.2
  289.7 8.2 %copy.141 = bf16[16,2,16,640]{2,1,0,3:T(2,128)(2,1)} copy(bf16[16,2,16,640]{3,2,1,0:T(8,128)(2,1)S(1)} %pad_maximum_fusion.6) | data formatting | bytes 1310720 | tf_op jit(solution)/shard_map/concatenate | solution.py:102
  301.2 8.4 %copy.143 = bf16[16,2,16,640]{2,1,0,3:T(2,128)(2,1)} copy(bf16[16,2,16,640]{3,2,1,0:T(8,128)(2,1)S(1)} %pad_maximum_fusion.7) | data formatting | bytes 1310720 | tf_op jit(solution)/shard_map/concatenate | solution.py:102
  312.8 8.4 %copy.145 = bf16[16,2,16,640]{2,1,0,3:T(2,128)(2,1)} copy(bf16[16,2,16,640]{3,2,1,0:T(8,128)(2,1)S(1)} %pad_maximum_fusion.8) | data formatting | bytes 1310720 | tf_op jit(solution)/shard_map/concatenate | solution.py:102
  321.2 5.8 %gather_fusion.1 = bf16[16,2,16,128]{2,1,3,0:T(2,128)(2,1)S(1)} fusion(bf16[16,2,16,640]{2,1,0,3:T(2,128)(2,1)} %copy.131, s32[16]{0:T(128)S(1)} %get-tuple-element.65), kind=kCustom, calls=%fused_computation.1 | custom fusion | bytes 262400 | tf_op jit(solution)/shard_map/vmap()/gather | solution.py:38
  328.8 5.8 %gather_fusion.2 = bf16[16,2,16,128]{2,1,3,0:T(2,128)(2,1)S(1)} fusion(bf16[16,2,16,640]{2,1,0,3:T(2,128)(2,1)} %copy.133, s32[16]{0:T(128)S(1)} %get-tuple-element.66), kind=kCustom, calls=%fused_computation.2 | custom fusion | bytes 262400 | tf_op jit(solution)/shard_map/vmap()/gather | solution.py:38
  336.5 5.8 %gather_fusion.3 = bf16[16,2,16,128]{2,1,3,0:T(2,128)(2,1)S(1)} fusion(bf16[16,2,16,640]{2,1,0,3:T(2,128)(2,1)} %copy.135, s32[16]{0:T(128)S(1)} %get-tuple-element.67), kind=kCustom, calls=%fused_computation.3 | custom fusion | bytes 262400 | tf_op jit(solution)/shard_map/vmap()/gather | solution.py:38
  344.1 6.0 %gather_fusion.4 = bf16[16,2,16,128]{2,1,3,0:T(2,128)(2,1)S(1)} fusion(bf16[16,2,16,640]{2,1,0,3:T(2,128)(2,1)} %copy.137, s32[16]{0:T(128)S(1)} %get-tuple-element.68), kind=kCustom, calls=%fused_computation.4 | custom fusion | bytes 262400 | tf_op jit(solution)/shard_map/vmap()/gather | solution.py:38
  352.0 5.8 %gather_fusion.5 = bf16[16,2,16,128]{2,1,3,0:T(2,128)(2,1)S(1)} fusion(bf16[16,2,16,640]{2,1,0,3:T(2,128)(2,1)} %copy.139, s32[16]{0:T(128)S(1)} %get-tuple-element.69), kind=kCustom, calls=%fused_computation.5 | custom fusion | bytes 262400 | tf_op jit(solution)/shard_map/vmap()/gather | solution.py:38
  359.6 5.8 %gather_fusion.6 = bf16[16,2,16,128]{2,1,3,0:T(2,128)(2,1)S(1)} fusion(bf16[16,2,16,640]{2,1,0,3:T(2,128)(2,1)} %copy.141, s32[16]{0:T(128)S(1)} %get-tuple-element.70), kind=kCustom, calls=%fused_computation.6 | custom fusion | bytes 262400 | tf_op jit(solution)/shard_map/vmap()/gather | solution.py:38
  367.2 6.1 %gather_fusion.7 = bf16[16,2,16,128]{2,1,3,0:T(2,128)(2,1)S(1)} fusion(bf16[16,2,16,640]{2,1,0,3:T(2,128)(2,1)} %copy.143, s32[16]{0:T(128)S(1)} %get-tuple-element.71), kind=kCustom, calls=%fused_computation.7 | custom fusion | bytes 262400 | tf_op jit(solution)/shard_map/vmap()/gather | solution.py:38
  375.1 5.8 %gather_fusion.8 = bf16[16,2,16,128]{2,1,3,0:T(2,128)(2,1)S(1)} fusion(bf16[16,2,16,640]{2,1,0,3:T(2,128)(2,1)} %copy.145, s32[16]{0:T(128)S(1)} %get-tuple-element.63), kind=kCustom, calls=%fused_computation.8 | custom fusion | bytes 262400 | tf_op jit(solution)/shard_map/vmap()/gather | solution.py:38
  382.8 19.8 %copy.146 = bf16[16,9,1,2,16,128]{5,4,3,2,1,0:T(8,128)(2,1)} copy(bf16[16,9,1,2,16,128]{4,3,5,0,1,2:T(2,128)(2,1)} %bitcast.212) | data formatting | bytes 2359296 | tf_op jit(solution)/shard_map/transpose | solution.py:18
  402.6 11.7 %all-to-all-start.1 = ((bf16[16,9,1,2,16,128]{5,4,3,2,1,0:T(8,128)(2,1)}), bf16[16,9,1,2,16,128]{5,4,3,2,1,0:T(8,128)(2,1)S(1)}, u32[]{:S(2)}, u32[]{:S(2)}) async-start(bf16[16,9,1,2,16,128]{5,4,3,2,1,0:T(8,128)(2,1)} %copy.146), calls=%async_computation.1 | async-start | bytes 2359296 | tf_op jit(solution)/shard_map/all_to_all | solution.py:23
  414.8 35.9 %all-to-all-done.1 = bf16[16,9,1,2,16,128]{5,4,3,2,1,0:T(8,128)(2,1)S(1)} async-done(((bf16[16,9,1,2,16,128]{5,4,3,2,1,0:T(8,128)(2,1)}), bf16[16,9,1,2,16,128]{5,4,3,2,1,0:T(8,128)(2,1)S(1)}, u32[]{:S(2)}, u32[]{:S(2)}) %all-to-all-start.1) | async-done | bytes 1179680 | tf_op jit(solution)/shard_map/all_to_all | solution.py:23
  455.4 33.1 %collective-permute-start.1 = (f32[1,2,16,128]{3,2,1,0:T(8,128)S(1)}, f32[1,2,16,128]{3,2,1,0:T(8,128)S(1)}, u32[]{:S(2)}, u32[]{:S(2)}) collective-permute-start(f32[1,2,16,128]{3,2,1,0:T(8,128)S(1)} %get-tuple-element.24), channel_id=1, source_target_pairs={{0,480},{16,496},{32,0},{48,16},{64,32},{80,48},{96,64},{112,80},{... | collective-permute-start | bytes 49160 | tf_op jit(solution)/shard_map/ppermute | solution.py:30
  490.4 8.5 %collective-permute-start.3 = (f32[1,2,16,128]{3,2,1,0:T(8,128)S(1)}, f32[1,2,16,128]{3,2,1,0:T(8,128)S(1)}, u32[]{:S(2)}, u32[]{:S(2)}) collective-permute-start(f32[1,2,16,128]{3,2,1,0:T(8,128)S(1)} %get-tuple-element.22), channel_id=1, source_target_pairs={{0,448},{16,464},{32,480},{48,496},{64,0},{80,16},{96,32},{112,48}... | collective-permute-start | bytes 49160 | tf_op jit(solution)/shard_map/ppermute | solution.py:30
  500.8 3.3 collective-permute-start.5
  506.4 3.5 collective-permute-start.7
  511.2 4.1 collective-permute-done.6
  (131 shorter events, 56.2 us)
Async XLA Ops:
  7.4 16.6 %copy-start.1 = (s32[512]{0:T(512)S(1)}, s32[512]{0:T(512)}, u32[]{:S(2)}) copy-start(s32[512]{0:T(512)} %param.9) | copy-start | bytes 6148
  7.4 16.6 %copy-start.2 = (s32[512]{0:T(512)S(1)}, s32[512]{0:T(512)}, u32[]{:S(2)}) copy-start(s32[512]{0:T(512)} %param.8) | copy-start | bytes 6148
  7.4 16.8 %copy-start.6 = (f32[128]{0:T(128)S(1)}, f32[128]{0:T(128)}, u32[]{:S(2)}) copy-start(f32[128]{0:T(128)} %param.12) | copy-start | bytes 1540
  7.5 16.8 %copy-start.3 = (s32[128]{0:T(128)S(1)}, s32[128]{0:T(128)}, u32[]{:S(2)}) copy-start(s32[128]{0:T(128)} %param.11) | copy-start | bytes 1540
  7.5 16.8 %copy-start.4 = (s32[128]{0:T(128)S(1)}, s32[128]{0:T(128)}, u32[]{:S(2)}) copy-start(s32[128]{0:T(128)} %param.10) | copy-start | bytes 1540
  7.5 16.8 %copy-start.5 = (f32[128]{0:T(128)S(1)}, f32[128]{0:T(128)}, u32[]{:S(2)}) copy-start(f32[128]{0:T(128)} %param.13) | copy-start | bytes 1540
  7.5 193.5 %all-to-all-start = ((bf16[2,4,512,512]{3,1,0,2:T(4,128)(2,1)}), bf16[2,4,512,512]{3,1,0,2:T(4,128)(2,1)}, u32[]{:S(2)}, u32[]{:S(2)}) async-start(bf16[2,4,512,512]{3,1,0,2:T(4,128)(2,1)} %copy.127), calls=%async_computation | async-start | bytes 8388608 | tf_op jit(solution)/shard_map/all_to_all | solution.py:79
  209.3 2.1 copy-start
  402.6 48.1 %all-to-all-start.1 = ((bf16[16,9,1,2,16,128]{5,4,3,2,1,0:T(8,128)(2,1)}), bf16[16,9,1,2,16,128]{5,4,3,2,1,0:T(8,128)(2,1)S(1)}, u32[]{:S(2)}, u32[]{:S(2)}) async-start(bf16[16,9,1,2,16,128]{5,4,3,2,1,0:T(8,128)(2,1)} %copy.146), calls=%async_computation.1 | async-start | bytes 2359296 | tf_op jit(solution)/shard_map/all_to_all | solution.py:23
  450.9 49.9 %collective-permute-start = (f32[1,2,16,128]{3,2,1,0:T(8,128)S(1)}, f32[1,2,16,128]{3,2,1,0:T(8,128)S(1)}, u32[]{:S(2)}, u32[]{:S(2)}) collective-permute-start(f32[1,2,16,128]{3,2,1,0:T(8,128)S(1)} %get-tuple-element.25), channel_id=1, source_target_pairs={{0,496},{16,0},{32,16},{48,32},{64,48},{80,64},{96,80},{112,96},{1... | collective-permute-start | bytes 49160 | tf_op jit(solution)/shard_map/ppermute | solution.py:30
  455.4 48.8 %collective-permute-start.1 = (f32[1,2,16,128]{3,2,1,0:T(8,128)S(1)}, f32[1,2,16,128]{3,2,1,0:T(8,128)S(1)}, u32[]{:S(2)}, u32[]{:S(2)}) collective-permute-start(f32[1,2,16,128]{3,2,1,0:T(8,128)S(1)} %get-tuple-element.24), channel_id=1, source_target_pairs={{0,480},{16,496},{32,0},{48,16},{64,32},{80,48},{96,64},{112,80},{... | collective-permute-start | bytes 49160 | tf_op jit(solution)/shard_map/ppermute | solution.py:30
  488.5 17.9 %collective-permute-start.2 = (f32[1,2,16,128]{3,2,1,0:T(8,128)S(1)}, f32[1,2,16,128]{3,2,1,0:T(8,128)S(1)}, u32[]{:S(2)}, u32[]{:S(2)}) collective-permute-start(f32[1,2,16,128]{3,2,1,0:T(8,128)S(1)} %get-tuple-element.23), channel_id=1, source_target_pairs={{0,464},{16,480},{32,496},{48,0},{64,16},{80,32},{96,48},{112,64},... | collective-permute-start | bytes 49160 | tf_op jit(solution)/shard_map/ppermute | solution.py:30
  490.4 19.4 %collective-permute-start.3 = (f32[1,2,16,128]{3,2,1,0:T(8,128)S(1)}, f32[1,2,16,128]{3,2,1,0:T(8,128)S(1)}, u32[]{:S(2)}, u32[]{:S(2)}) collective-permute-start(f32[1,2,16,128]{3,2,1,0:T(8,128)S(1)} %get-tuple-element.22), channel_id=1, source_target_pairs={{0,448},{16,464},{32,480},{48,496},{64,0},{80,16},{96,32},{112,48}... | collective-permute-start | bytes 49160 | tf_op jit(solution)/shard_map/ppermute | solution.py:30
  498.9 11.0 %collective-permute-start.4 = (f32[1,2,16,128]{3,2,1,0:T(8,128)S(1)}, f32[1,2,16,128]{3,2,1,0:T(8,128)S(1)}, u32[]{:S(2)}, u32[]{:S(2)}) collective-permute-start(f32[1,2,16,128]{3,2,1,0:T(8,128)S(1)} %get-tuple-element.21), channel_id=1, source_target_pairs={{0,432},{16,448},{32,464},{48,480},{64,496},{80,0},{96,16},{112,32... | collective-permute-start | bytes 49160 | tf_op jit(solution)/shard_map/ppermute | solution.py:30
  500.8 10.4 %collective-permute-start.5 = (f32[1,2,16,128]{3,2,1,0:T(8,128)S(1)}, f32[1,2,16,128]{3,2,1,0:T(8,128)S(1)}, u32[]{:S(2)}, u32[]{:S(2)}) collective-permute-start(f32[1,2,16,128]{3,2,1,0:T(8,128)S(1)} %get-tuple-element.20), channel_id=1, source_target_pairs={{0,416},{16,432},{32,448},{48,464},{64,480},{80,496},{96,0},{112,1... | collective-permute-start | bytes 49160 | tf_op jit(solution)/shard_map/ppermute | solution.py:30
  504.2 11.1 %collective-permute-start.6 = (f32[1,2,16,128]{3,2,1,0:T(8,128)S(1)}, f32[1,2,16,128]{3,2,1,0:T(8,128)S(1)}, u32[]{:S(2)}, u32[]{:S(2)}) collective-permute-start(f32[1,2,16,128]{3,2,1,0:T(8,128)S(1)} %get-tuple-element.19), channel_id=1, source_target_pairs={{0,400},{16,416},{32,432},{48,448},{64,464},{80,480},{96,496},{112... | collective-permute-start | bytes 49160 | tf_op jit(solution)/shard_map/ppermute | solution.py:30
  506.4 8.9 %collective-permute-start.7 = (f32[1,2,16,128]{3,2,1,0:T(8,128)S(1)}, f32[1,2,16,128]{3,2,1,0:T(8,128)S(1)}, u32[]{:S(2)}, u32[]{:S(2)}) collective-permute-start(f32[1,2,16,128]{3,2,1,0:T(8,128)S(1)} %get-tuple-element.18), channel_id=1, source_target_pairs={{0,384},{16,400},{32,416},{48,432},{64,448},{80,464},{96,480},{112... | collective-permute-start | bytes 49160 | tf_op jit(solution)/shard_map/ppermute | solution.py:30
where the time goes:
time: 525 us; the launch traced here: 517 us
  waiting for transfers between devices  216 us (41%)
  local copies, waits for them, and re-layouts  185 us (35%)
  starting transfers between devices  84.3 us (16%)
  matrix products  25.8 us (5%)
    all_to_all x1, waiting for transfers between devices, local(): lax.all_to_all(smatrix, 'tile', split_axis=2, concat_axis=1, tiled=True)  175 us
    concatenate x9, local copies, waits for them, and re-layouts, owner_block(): extended = jnp.concatenate([waves, waves[:, :, :, :CROP]], axis=3)  74.8 us
    ppermute x8, starting transfers between devices, passed_along(): return lax.ppermute(value, axis, pairs)  56.2 us
    gather x9, local copies, waits for them, and re-layouts, cut_columns(): return lax.dynamic_slice_in_dim(piece, begin, CROP, 2)  53 us
    all_to_all x1, waiting for transfers between devices, sum_at_owner(): lax.all_to_all(parts, axis, split_axis=0, concat_axis=0, tiled=True)  35.9 us
    unnamed x40, local copies, waits for them, and re-layouts  29.7 us
    dot_general x9, matrix products, owner_block(): jnp.dot(mixing, stacked, preferred_element_type=jnp.float32)  25 us
    transpose x1, local copies, waits for them, and re-layouts, cut_along(): return jnp.moveaxis(shard.reshape(*before, size, -1, *after), dim, 0)  19.8 us
  transfers between devices with their start and end apart: 10, of which 4 were waited for; matrix products, arithmetic and copies ran while one was open for 1% of the time, Pallas kernels for 0%

commit v1 on v0

v1 whole, which is shorter than its diff:
```python
import math

import jax
import jax.numpy as jnp
from jax import lax
from jax.experimental import pallas as pl
from jax.experimental.pallas import tpu as pltpu
from jax.sharding import Mesh
from jax.sharding import PartitionSpec as P

CROP = 128
STRIP = 16
FIELD = 512
PLANES = 4
TILES = 8
STRIPS = 4
SOURCES = 8
DEPTH = 64

two_pi = 2.0 * math.pi


def mix_kernel(strips_ref, weight_ref, tile_ref, out_ref, wide, rows):
    def strip(r, carry):
        for k in range(PLANES):
            wide[k] = strips_ref[r, :, k * CROP : (k + 1) * CROP].astype(jnp.float32)

        def one_row(i, inner):
            field_row = jnp.concatenate(
                [wide[k, pl.ds(i, DEPTH, stride=STRIP), :].astype(jnp.bfloat16) for k in range(PLANES)], axis=1
            )
            full = jnp.dot(weight_ref[r], field_row, preferred_element_type=jnp.float32)
            place = tile_ref[r]
            picked = jnp.where(
                place < 2,
                jnp.where(place == 0, full[:, :128], full[:, 128:256]),
                jnp.where(place == 2, full[:, 256:384], full[:, 384:]),
            )
            rows[pl.ds(i, full.shape[0], stride=STRIP), :] = picked
            return inner

        lax.fori_loop(0, STRIP, one_row, 0)
        out_ref[r] = rows[...].astype(jnp.bfloat16)
        return carry

    lax.fori_loop(0, STRIPS, strip, 0)


def mix(strips, weights, tiles):
    count = weights.shape[1]
    return pl.pallas_call(
        mix_kernel,
        out_shape=jax.ShapeDtypeStruct((STRIPS, count * STRIP, CROP), jnp.bfloat16),
        in_specs=[pl.BlockSpec(memory_space=pltpu.VMEM)] * 3,
        out_specs=pl.BlockSpec(memory_space=pltpu.VMEM),
        scratch_shapes=[
            pltpu.VMEM((PLANES, DEPTH * STRIP, CROP), jnp.float32),
            pltpu.VMEM((count * STRIP, CROP), jnp.float32),
        ],
        compiler_params=pltpu.CompilerParams(vmem_limit_bytes=48 * 2**20),
    )(strips, weights, tiles)


def transform(exit_re, exit_im):
    places = jnp.arange(CROP, dtype=jnp.int32)
    ticks = places[:, None] * places[None, :] % CROP
    angle = two_pi * ticks.astype(jnp.float32) / CROP
    norm_factor = 1.0 / math.sqrt(CROP)
    table_re = jnp.cos(angle) * norm_factor
    table_im = -jnp.sin(angle) * norm_factor

    def dot(a, b):
        return jnp.dot(a, b, precision=lax.Precision.HIGHEST)

    half_re = dot(exit_re, table_re) - dot(exit_im, table_im)
    half_im = dot(exit_re, table_im) + dot(exit_im, table_re)
    full_re = dot(table_re, half_re) - dot(table_im, half_im)
    full_im = dot(table_re, half_im) + dot(table_im, half_re)
    return full_re * full_re + full_im * full_im


def per_strip(values, x, c):
    ny, nzh = values.shape[2:4]
    own = lax.dynamic_index_in_dim(values, x, 0, False)
    before = lax.dynamic_index_in_dim(values, (x + PLANES - 1) % PLANES, 0, False)
    s = STRIPS * c + jnp.arange(STRIPS)
    zl = jnp.arange(TILES)
    main = jnp.where((zl[None, :] <= s[:, None])[:, :, None, None, None], own[None], before[None])
    extra = lax.dynamic_slice_in_dim(before, STRIPS * c, STRIPS, 0)
    main = main.transpose(0, 2, 3, 1, 4).reshape(STRIPS, ny, nzh * TILES * 2)
    return jnp.concatenate([main, extra.reshape(STRIPS, ny, nzh * 2)], axis=2)


def local(smatrix, offset_y, offset_x, beam_qx, beam_qy, beam_amp, beam_phase):
    x, zl, c = (lax.axis_index(a) for a in ("x", "zl", "c"))
    y, zh = lax.axis_index("y"), lax.axis_index("zh")
    ny, nzh = lax.axis_size("y"), lax.axis_size("zh")
    nz = nzh * TILES
    beams = BEAMS_PER
    total = beam_qx.shape[0] * ny * nzh * 2

    params = jnp.stack([beam_qx.astype(jnp.float32), beam_qy.astype(jnp.float32), beam_amp, beam_phase])
    params = lax.dynamic_index_in_dim(params.reshape(4, PLANES, TILES, beams), zl, 2, False)
    params = lax.all_gather(params, "c", axis=2)
    params = jnp.broadcast_to(params[:, :, :, None, :], (4, PLANES, 2, 2, beams)).reshape(4, DEPTH)
    qx, qy = params[0].astype(jnp.int32), params[1].astype(jnp.int32)
    amp, phase = params[2] * (1.0 / math.sqrt(total)), params[3]
    part = jnp.arange(DEPTH) // beams % 2

    grid = (PLANES, TILES, ny, nzh, 2)
    first_y = per_strip(offset_y.reshape(grid), x, c)
    first_x = per_strip(offset_x.reshape(grid), x, c)
    turns = (first_x + CROP // 2)[..., None] * qx + (first_y + CROP // 2)[..., None] * qy
    quarter = (jnp.arange(2)[:, None] - part[None, :]) * (FIELD // 4)
    turns = (turns[..., None, :] + quarter) % FIELD
    weights = (amp * jnp.cos(phase - two_pi * turns.astype(jnp.float32) / FIELD)).astype(jnp.bfloat16)
    count = first_x.shape[1] * first_x.shape[2] * 2
    weights = weights.reshape(STRIPS, count, DEPTH)
    lanes = jnp.arange(CROP)
    tiles = (first_x[..., None] // CROP + (lanes < (first_x % CROP)[..., None])) % PLANES
    tiles = jnp.broadcast_to(tiles[..., None, :], (*first_x.shape, 2, CROP)).reshape(STRIPS, count, CROP)

    split = smatrix.reshape(2, beams, SOURCES, STRIPS, STRIP, FIELD)
    strips = lax.all_to_all(split, ("x", "c"), split_axis=2, concat_axis=0)
    strips = strips.transpose(3, 0, 1, 2, 4, 5).reshape(STRIPS, DEPTH * STRIP, FIELD)
    waves = mix(strips, weights, tiles)

    each = count // ny
    waves = waves.reshape(STRIPS, ny, each, STRIP, CROP)
    waves = lax.psum_scatter(waves, "y", scatter_dimension=1)
    main = waves[:, : nz * 4].reshape(STRIPS, nzh, TILES, 4, STRIP, CROP).transpose(1, 2, 0, 3, 4, 5)
    extra = waves[:, nz * 4 :].reshape(STRIPS, nzh, 4, STRIP, CROP).transpose(1, 0, 2, 3, 4)
    empty = jnp.zeros_like(extra)
    extra = jnp.where(c == 0, jnp.concatenate([extra, empty], 1), jnp.concatenate([empty, extra], 1))
    both = jnp.concatenate([main, extra[:, :, None]], axis=2).reshape(nz, STRIPS + 1, 4, STRIP, CROP)
    both = lax.psum_scatter(both, ("zh", "zl"), scatter_dimension=0).astype(jnp.float32)
    both = both.reshape(STRIPS + 1, 2, 2, STRIP, CROP).transpose(1, 0, 2, 3, 4)

    s = STRIPS * c + jnp.arange(STRIPS)
    flat = ((y * nzh + zh) * 2 + jnp.arange(2)).astype(jnp.int32)
    per_tile = ny * nzh * 2
    own_y = lax.dynamic_slice_in_dim(offset_y, (x * TILES + zl) * per_tile + flat[0], 2) % STRIP
    before_y = lax.dynamic_slice_in_dim(offset_y, (((x + PLANES - 1) % PLANES) * TILES + zl) * per_tile + flat[0], 2) % STRIP
    i = jnp.arange(STRIP)
    own_row = (s[None, :, None] * STRIP + i >= zl * STRIP + own_y[:, None, None])[:, :, None, :, None]
    own = jnp.where(own_row, both[:, :STRIPS], 0.0)
    below = (s < zl)[None, :, None, None, None]
    cut = (s == zl)[None, :, None, None, None] & (i < before_y[:, None])[:, None, None, :, None]
    before = jnp.where(below, both[:, :STRIPS], jnp.where(cut, both[:, STRIPS:], 0.0))

    def pick(pair, core):
        return lax.dynamic_index_in_dim(pair, core, 0, False)

    def sent(value, dx, flip):
        pairs = [
            (a * 2 + b, ((a - dx) % PLANES) * 2 + (b ^ flip)) for a in range(PLANES) for b in range(2)
        ]
        return lax.ppermute(value, ("x", "c"), pairs)

    same = pick(own, c) + sent(pick(before, c), 1, 0)
    other = sent(pick(own, 1 - c), 0, 1) + sent(pick(before, 1 - c), 1, 1)
    first, second = jnp.where(c == 0, same, other), jnp.where(c == 0, other, same)
    wave = jnp.concatenate([first, second], axis=0)
    wave = wave.transpose(1, 0, 2, 3).reshape(2, CROP, CROP)
    return transform(wave[0], wave[1])[None]


BEAMS_PER = 4


def solution(mesh):
    tile, beam = mesh.shape["tile"], mesh.shape["beam"]
    del tile
    shape = (PLANES, TILES, beam // 4 if beam >= 4 else 1, 2 if beam >= 4 else 1, 2)
    fine = Mesh(mesh.devices.reshape(shape), ("x", "zl", "y", "zh", "c"))
    group = ("y", "zh", "c")
    return jax.shard_map(
        local,
        mesh=fine,
        in_specs=(P(None, (*group, "x", "zl"), None, None), P(), P(), P(group), P(group), P(group), P(group)),
        out_specs=P(("x", "zl", *group), None, None),
        check_vma=False,
    )
```

time: 525 us -> 326 us (0.62); the launches traced: 517 us -> 326 us
  local copies, waits for them, and re-layouts: 185 us -> 22.2 us
  starting transfers between devices: 84.3 us -> 30.7 us
  matrix products: 25.8 us -> 4.28 us
  Pallas kernels: 0 us -> 21.5 us
  waiting for transfers between devices: 216 us -> 227 us
  between operations: 3.49 us -> 14 us
    all_to_all x2 -> x1, waiting for transfers between devices: 211 us -> 40.4 us  [local(): strips = lax.all_to_all(split, ('x', 'c'), split_axis=2, concat_axis=0)]
    unnamed x0 -> x3, waiting for transfers between devices: none -> 129 us
    concatenate x10 -> x2, local copies, waits for them, and re-layouts: 74.8 us -> 0.23 us  [per_strip(): return jnp.concatenate([main, extra.reshape(STRIPS, ny, nzh * 2)], axis=2)]
    reduce_scatter x0 -> x1, waiting for transfers between devices: none -> 56.4 us  [local(): waves = lax.psum_scatter(waves, 'y', scatter_dimension=1)]
    gather x9 -> x0, local copies, waits for them, and re-layouts: 53 us -> none  [cut_columns(): return lax.dynamic_slice_in_dim(piece, begin, CROP, 2)]
    ppermute x8 -> x3, starting transfers between devices: 56.2 us -> 19.2 us  [sent(): return lax.ppermute(value, ('x', 'c'), pairs)]
    unnamed x40 -> x14, local copies, waits for them, and re-layouts: 29.7 us -> 2.84 us
    pallas_call x0 -> x1, Pallas kernels: none -> 21.5 us  [mix(): pl.pallas_call(mix_kernel, out_shape=jax.ShapeDtypeStruct((STRIPS, count...]
  transfers between devices with their start and end apart: 10 -> 6, of which waited for: 4 -> 4; matrix products, arithmetic and copies ran while one was open for 1% -> 3% of each run, Pallas kernels for 0% -> 0%
where the time goes in v1:
time: 326 us
  waiting for transfers between devices  227 us (70%)
  starting transfers between devices  30.7 us (9%)
  local copies, waits for them, and re-layouts  22.2 us (7%)
  Pallas kernels  21.5 us (7%)
  between operations  14 us (4%)
  other arithmetic  4.78 us (1%)
  matrix products  4.28 us (1%)
    unnamed x3, waiting for transfers between devices  129 us
    reduce_scatter x1, waiting for transfers between devices, local(): waves = lax.psum_scatter(waves, 'y', scatter_dimension=1)  56.4 us
    all_to_all x1, waiting for transfers between devices, local(): strips = lax.all_to_all(split, ('x', 'c'), split_axis=2, concat_axis=0)  40.4 us
    pallas_call x1, Pallas kernels, mix(): pl.pallas_call(mix_kernel, out_shape=jax.ShapeDtypeStruct((STRIPS, count...  21.5 us
    ppermute x3, starting transfers between devices, sent(): return lax.ppermute(value, ('x', 'c'), pairs)  19.2 us
    all_to_all x1, starting transfers between devices, local(): strips = lax.all_to_all(split, ('x', 'c'), split_axis=2, concat_axis=0)  11.5 us
  transfers between devices with their start and end apart: 6, of which 4 were waited for; matrix products, arithmetic and copies ran while one was open for 3% of the time, Pallas kernels for 0%

profile of v1, /device:TPU:1, one launch (start us, length us, event | category | flops | bytes accessed | tf_op | source)
XLA Modules:
  0.0 326.0 jit_solution(7774869776432272882)
XLA Ops:
  6.5 4.8 %copy.83 = bf16[1,2,4,8,4,16,512]{6,5,2,1,4,0,3:T(8,128)(2,1)} copy(bf16[1,2,4,8,4,16,512]{6,5,4,3,2,1,0:T(8,128)(2,1)} %bitcast.96) | data formatting | bytes 8388608 | tf_op jit(solution)/shard_map/broadcast_in_dim;reshape | solution.py:124
  11.4 11.5 %all-to-all-start = ((bf16[1,2,4,8,4,16,512]{6,5,2,1,4,0,3:T(8,128)(2,1)}), bf16[1,2,4,8,4,16,512]{6,5,2,1,4,0,3:T(8,128)(2,1)}, u32[]{:S(2)}, u32[]{:S(2)}) async-start(bf16[1,2,4,8,4,16,512]{6,5,2,1,4,0,3:T(8,128)(2,1)} %copy.83), calls=%async_computation | async-start | bytes 8388608 | tf_op jit(solution)/shard_map/all_to_all | solution.py:124
  22.9 0.2 reshape.406
  23.1 0.2 reshape.407
  25.9 1.8 all_gather.4
  28.4 0.2 add_select_fusion.1
  28.7 0.2 multiply_add_fusion
  29.2 2.3 fusion.10.weight_ref
  31.4 40.4 %all-to-all-done = bf16[1,2,4,8,4,16,512]{6,5,2,1,4,0,3:T(8,128)(2,1)} async-done(((bf16[1,2,4,8,4,16,512]{6,5,2,1,4,0,3:T(8,128)(2,1)}), bf16[1,2,4,8,4,16,512]{6,5,2,1,4,0,3:T(8,128)(2,1)}, u32[]{:S(2)}, u32[]{:S(2)}) %all-to-all-start) | async-done | bytes 4194336 | tf_op jit(solution)/shard_map/all_to_all | solution.py:124
  71.8 3.0 copy.84
  74.8 0.2 broadcast_in_dim.188
  75.0 21.5 %shard_map.73 = bf16[4,4608,128]{2,1,0:T(8,128)(2,1)} custom-call(bf16[4,1024,512]{2,1,0:T(8,128)(2,1)S(1)} %bitcast.93, bf16[4,288,64]{2,1,0:T(8,128)(2,1)S(1)} %fusion.10.weight_ref, s32[4,288,128]{2,1,0:T(8,128)S(1)} %bitcast.94), custom_call_target="tpu_custom_call" | custom-call | tf_op jit(solution)/shard_map/pallas_call | solution.py:51
  96.5 5.5 %copy.106 = bf16[4,4,72,16,128]{4,3,2,0,1:T(8,128)(2,1)} copy(bf16[4,4,72,16,128]{4,3,2,1,0:T(8,128)(2,1)} %bitcast.95) | data formatting | bytes 9437184 | tf_op jit(solution)/shard_map/reshape | solution.py:129
  102.1 56.4 %reduce-scatter.5.cloned.1.call-done = bf16[4,1,72,16,128]{4,3,2,0,1:T(8,128)(2,1)} async-done(((bf16[4,4,72,16,128]{4,3,2,0,1:T(8,128)(2,1)}), bf16[4,1,72,16,128]{4,3,2,0,1:T(8,128)(2,1)}) %reduce-scatter.5.cloned.1.call-update) | async-done | bytes 1179664 | tf_op jit(solution)/shard_map/reduce_scatter | solution.py:130
  158.5 1.4 slice.63
  159.9 0.9 slice.64
  160.8 1.2 pad_maximum_fusion
  162.2 1.3 dynamic-slice.4
  163.8 128.8 %all-reduce.5.cloned.1.call-done = bf16[16,5,4,16,128]{4,3,2,0,1:T(8,128)(2,1)} async-done(((bf16[16,5,4,16,128]{4,3,2,0,1:T(8,128)(2,1)}), bf16[16,5,4,16,128]{4,3,2,0,1:T(8,128)(2,1)}) %all-reduce.5.cloned.1.call-update) | async-done | bytes 1310736
  292.6 1.5 constant_dynamic-slice_fusion.6
  294.3 4.3 %collective-permute-start = (f32[4,2,16,128]{3,2,1,0:T(8,128)S(1)}, f32[4,2,16,128]{3,2,1,0:T(8,128)S(1)}, u32[]{:S(2)}, u32[]{:S(2)}) collective-permute-start(f32[4,2,16,128]{3,2,1,0:T(8,128)S(1)} %get-tuple-element.11), channel_id=1, source_target_pairs={{0,384},{1,385},{128,0},{129,1},{256,128},{257,129},{384,256},{385... | collective-permute-start | bytes 196616 | tf_op jit(solution)/shard_map/ppermute | solution.py:158
  298.6 12.9 %collective-permute-start.2 = (f32[4,2,16,128]{3,2,1,0:T(8,128)S(1)}, f32[4,2,16,128]{3,2,1,0:T(8,128)S(1)}, u32[]{:S(2)}, u32[]{:S(2)}) collective-permute-start(f32[4,2,16,128]{3,2,1,0:T(8,128)S(1)} %get-tuple-element.12), channel_id=1, source_target_pairs={{0,385},{1,384},{128,1},{129,0},{256,129},{257,128},{384,257},{385... | collective-permute-start | bytes 196616 | tf_op jit(solution)/shard_map/ppermute | solution.py:158
  311.6 1.9 collective-permute-start.1
  313.5 1.2 collective-permute-done.1
  314.8 0.5 fusion.29
  315.3 0.5 fusion.20
  315.7 0.5 convolution_add_fusion.1
  316.2 0.5 fusion.18
  316.6 0.5 convolution_subtract_fusion.1
  317.1 0.5 fusion.19
  317.6 0.5 fusion.3
  318.0 1.1 fusion.2
  (83 shorter events, 4.1 us)
Async XLA Ops:
  11.4 11.5 %copy-start.1 = (s32[512]{0:T(512)S(1)}, s32[512]{0:T(512)}, u32[]{:S(2)}) copy-start(s32[512]{0:T(512)} %param.9) | copy-start | bytes 6148
  11.4 11.7 %copy-start = (s32[512]{0:T(512)S(1)}, s32[512]{0:T(512)}, u32[]{:S(2)}) copy-start(s32[512]{0:T(512)} %param.8) | copy-start | bytes 6148
  11.4 14.1 %copy-start.4 = (s32[128]{0:T(128)S(1)}, s32[128]{0:T(128)}, u32[]{:S(2)}) copy-start(s32[128]{0:T(128)} %param.10) | copy-start | bytes 1540
  11.4 14.2 %copy-start.5 = (s32[128]{0:T(128)S(1)}, s32[128]{0:T(128)}, u32[]{:S(2)}) copy-start(s32[128]{0:T(128)} %param.11) | copy-start | bytes 1540
  11.4 14.3 %copy-start.2 = (f32[128]{0:T(128)S(1)}, f32[128]{0:T(128)}, u32[]{:S(2)}) copy-start(f32[128]{0:T(128)} %param.12) | copy-start | bytes 1540
  11.4 14.4 %copy-start.3 = (f32[128]{0:T(128)S(1)}, f32[128]{0:T(128)}, u32[]{:S(2)}) copy-start(f32[128]{0:T(128)} %param.13) | copy-start | bytes 1540
  11.4 60.4 %all-to-all-start = ((bf16[1,2,4,8,4,16,512]{6,5,2,1,4,0,3:T(8,128)(2,1)}), bf16[1,2,4,8,4,16,512]{6,5,2,1,4,0,3:T(8,128)(2,1)}, u32[]{:S(2)}, u32[]{:S(2)}) async-start(bf16[1,2,4,8,4,16,512]{6,5,2,1,4,0,3:T(8,128)(2,1)} %copy.83), calls=%async_computation | async-start | bytes 8388608 | tf_op jit(solution)/shard_map/all_to_all | solution.py:124
  22.9 135.6 %reduce-scatter.5.cloned.1.call-start = ((), (), s32[]{:S(2)}) async-start(), calls=%async_computation.2 | async-start | bytes 5898240 | tf_op jit(solution)/shard_map/reduce_scatter | solution.py:130
  102.0 190.6 %all-reduce.5.cloned.1.call-start = ((), (), s32[]{:S(2)}) async-start(), calls=%async_computation.3 | async-start | bytes 2621440
  294.3 19.2 %collective-permute-start = (f32[4,2,16,128]{3,2,1,0:T(8,128)S(1)}, f32[4,2,16,128]{3,2,1,0:T(8,128)S(1)}, u32[]{:S(2)}, u32[]{:S(2)}) collective-permute-start(f32[4,2,16,128]{3,2,1,0:T(8,128)S(1)} %get-tuple-element.11), channel_id=1, source_target_pairs={{0,384},{1,385},{128,0},{129,1},{256,128},{257,129},{384,256},{385... | collective-permute-start | bytes 196616 | tf_op jit(solution)/shard_map/ppermute | solution.py:158
  298.6 14.9 %collective-permute-start.2 = (f32[4,2,16,128]{3,2,1,0:T(8,128)S(1)}, f32[4,2,16,128]{3,2,1,0:T(8,128)S(1)}, u32[]{:S(2)}, u32[]{:S(2)}) collective-permute-start(f32[4,2,16,128]{3,2,1,0:T(8,128)S(1)} %get-tuple-element.12), channel_id=1, source_target_pairs={{0,385},{1,384},{128,1},{129,0},{256,129},{257,128},{384,257},{385... | collective-permute-start | bytes 196616 | tf_op jit(solution)/shard_map/ppermute | solution.py:158
  311.6 3.1 collective-permute-start.1
Sparse Core Ops, SparseCore 0:
  102.1 56.2 reduce-scatter.4
  162.2 130.3 all-reduce.4

commit v2 on v1

v2 whole, which is shorter than its diff:
```python
import functools
import math

import jax
import jax.numpy as jnp
import numpy as np
from jax import lax
from jax.experimental import pallas as pl
from jax.experimental.pallas import tpu as pltpu
from jax.sharding import Mesh
from jax.sharding import PartitionSpec as P

CROP = 128
STRIP = 16
FIELD = 512
PLANES = 4
TILES = 8
STRIPS = 4
SOURCES = 8
DEPTH = 64

two_pi = 2.0 * math.pi


def remote(source, target, send_sem, recv_sem, device):
    return pltpu.make_async_remote_copy(
        src_ref=source,
        dst_ref=target,
        send_sem=send_sem,
        recv_sem=recv_sem,
        device_id=device,
        device_id_type=pl.DeviceIdType.MESH,
    )


def loop(start, stop, body):
    def step(i, carry):
        body(i)
        return carry

    lax.fori_loop(start, stop, step, 0)


def probe_kernel(
    ny,
    nzh,
    smatrix,
    weight_ref,
    tile_ref,
    own_mask,
    cut_mask,
    dft,
    out_ref,
    raw,
    wide,
    rows,
    waves,
    ywave,
    summed,
    zwave,
    ewave,
    extra,
    own_part,
    low_part,
    last,
    full,
    local_sem,
    a_send,
    a_recv,
    y_send,
    y_recv,
    z_send,
    z_recv,
    e_send,
    e_recv,
    f_send,
    f_recv,
):
    x, zl, y, zh, c = (lax.axis_index(a) for a in ("x", "zl", "y", "zh", "c"))
    nz = nzh * TILES
    each = nz * 4 + nzh * 4
    z = zh * TILES + zl
    me = x * 2 + c
    before_x = lax.rem(x + PLANES - 1, PLANES)

    def peer(d):
        p = lax.rem(me + d, SOURCES)
        return p, {"x": p // 2, "c": lax.rem(p, 2)}

    def zpeer(d):
        p = lax.rem(z + d, nz)
        return p, {"zh": p // TILES, "zl": lax.rem(p, TILES)}

    def ypeer(d):
        p = lax.rem(y + d, ny)
        return p, {"y": p}

    def greet(peers, count):
        def one(d):
            pl.semaphore_signal(
                pltpu.get_barrier_semaphore(), inc=1, device_id=peers(d)[1], device_id_type=pl.DeviceIdType.MESH
            )

        loop(1, count, one)

    greet(peer, SOURCES)
    greet(ypeer, ny)
    greet(zpeer, nz)
    pl.semaphore_wait(pltpu.get_barrier_semaphore(), SOURCES + ny + nz - 3)

    def part_rows(p, r):
        return smatrix.at[:, pl.ds(pl.multiple_of(p * (STRIPS * STRIP) + r * STRIP, STRIP), STRIP), :]

    def raw_copy(d, r):
        p, device = peer(d)
        return remote(part_rows(p, r), raw.at[r, me], a_send.at[r, p], a_recv.at[r, me], device)

    def raw_own(r):
        return pltpu.make_async_copy(part_rows(me, r), raw.at[r, me], local_sem.at[r])

    def raw_start(r):
        loop(1, SOURCES, lambda d: raw_copy(d, r).start())
        raw_own(r).start()

    loop(0, STRIPS, raw_start)

    def raw_wait(d, r):
        p, device = peer(d)
        remote(raw.at[r, p], raw.at[r, p], a_send.at[r, p], a_recv.at[r, p], device).wait_recv()

    def y_copy(d, r):
        p, device = ypeer(d)
        return remote(waves.at[r, p], ywave.at[r, y], y_send.at[r, p], y_recv.at[r, y], device)

    def y_wait(d, r):
        p, device = ypeer(d)
        remote(ywave.at[r, p], ywave.at[r, p], y_send.at[r, p], y_recv.at[r, p], device).wait_recv()

    def z_copy(d, r):
        p, device = zpeer(d)
        return remote(summed.at[r, pl.ds(p * 4, 4)], zwave.at[r, z], z_send.at[r, p], z_recv.at[r, z], device)

    def z_wait(d, r):
        p, device = zpeer(d)
        remote(zwave.at[r, p], zwave.at[r, p], z_send.at[r, p], z_recv.at[r, p], device).wait_recv()

    def e_copy(h, r):
        return remote(
            summed.at[r, pl.ds((nz + h) * 4, 4)],
            ewave.at[z],
            e_send.at[r, h],
            e_recv.at[z],
            {"zh": h, "zl": c * STRIPS + r},
        )

    def e_each(r, act):
        def one(h):
            @pl.when(h * TILES + c * STRIPS + r != z)
            def _():
                act(e_copy(h, r))

        loop(0, nzh, one)

    def mixing(r):
        raw_own(r).wait()
        loop(1, SOURCES, lambda d: raw_wait(d, r))

        def widen(p):
            for k in range(PLANES):
                part = raw[r, p, :, :, k * CROP : (k + 1) * CROP].astype(jnp.float32)
                wide[k, pl.ds(pl.multiple_of(p * 128, 128), 128), :] = part.reshape(128, CROP)

        loop(0, SOURCES, widen)

        def one_row(i):
            field_row = jnp.concatenate(
                [wide[k, pl.ds(i, DEPTH, stride=STRIP), :].astype(jnp.bfloat16) for k in range(PLANES)], axis=1
            )
            product = jnp.dot(weight_ref[r], field_row, preferred_element_type=jnp.float32)
            place = tile_ref[r]
            picked = jnp.where(
                place < 2,
                jnp.where(place == 0, product[:, :128], product[:, 128:256]),
                jnp.where(place == 2, product[:, 256:384], product[:, 384:]),
            )
            rows[pl.ds(i, ny * each, stride=STRIP), :] = picked

        loop(0, STRIP, one_row)

        def narrow(p):
            size = each * STRIP
            part = rows[pl.ds(pl.multiple_of(p * size, STRIP), size), :].astype(jnp.bfloat16)
            waves[r, p] = part.reshape(each, STRIP, CROP)

        loop(0, ny, narrow)
        loop(1, ny, lambda d: y_copy(d, r).start())

    def summing(r):
        loop(1, ny, lambda d: y_wait(d, r))

        def block(b):
            at = pl.ds(b * 4, 4)
            total = waves[r, y, at].astype(jnp.float32)
            for d in range(1, ny):
                total += ywave[r, ypeer(d)[0], at].astype(jnp.float32)
            summed[r, at] = total.astype(jnp.bfloat16)

        loop(0, each // 4, block)
        loop(1, nz, lambda d: z_copy(d, r).start())
        e_each(r, lambda copy: copy.start())

    def stage(r):
        mixing(r)

        @pl.when(r > 0)
        def _():
            summing(r - 1)

    loop(0, STRIPS, stage)
    summing(STRIPS - 1)

    extra[...] = jnp.zeros_like(extra)

    @pl.when(zl // STRIPS == c)
    def _():
        def e_wait(d):
            p, device = zpeer(d)
            remote(ewave.at[p], ewave.at[p], e_send.at[0, 0], e_recv.at[p], device).wait_recv()

        loop(1, nz, e_wait)
        total = summed[lax.rem(zl, STRIPS), pl.ds((nz + zh) * 4, 4)].astype(jnp.float32)
        for d in range(1, nz):
            total += ewave[zpeer(d)[0]].astype(jnp.float32)
        extra[...] = total

    def closing(r):
        loop(1, nz, lambda d: z_wait(d, r))
        total = summed[r, pl.ds(z * 4, 4)].astype(jnp.float32)
        for d in range(1, nz):
            total += zwave[r, zpeer(d)[0]].astype(jnp.float32)
        s = c * STRIPS + r
        low = jnp.where(s < zl, 1.0, 0.0)
        cut = jnp.where(s == zl, 1.0, 0.0)
        for k in range(2):
            for part in range(2):
                value = total[2 * k + part]
                own_part[k, r, part] = value * own_mask[k, r]
                low_part[k, r, part] = value * low + extra[2 * k + part] * cut_mask[k] * cut

    loop(0, STRIPS, closing)

    other = 1 - c
    finals = [
        remote(own_part.at[other], last.at[0], f_send.at[0], f_recv.at[0], {"c": other}),
        remote(low_part.at[c], last.at[1], f_send.at[1], f_recv.at[1], {"x": before_x}),
        remote(low_part.at[other], last.at[2], f_send.at[2], f_recv.at[2], {"x": before_x, "c": other}),
    ]
    for copy in finals:
        copy.start()
    for copy in finals:
        copy.wait_recv()
    for r in range(STRIPS):
        for part in range(2):
            full[part, c * STRIPS + r] = own_part[c, r, part] + last[1, r, part]
            full[part, other * STRIPS + r] = last[0, r, part] + last[2, r, part]

    def dot(a, b):
        return jnp.dot(a, b, precision=lax.Precision.HIGHEST, preferred_element_type=jnp.float32)

    exit_re, exit_im = full[0].reshape(CROP, CROP), full[1].reshape(CROP, CROP)
    table_re, table_im = dft[0], dft[1]
    half_re = dot(exit_re, table_re) - dot(exit_im, table_im)
    half_im = dot(exit_re, table_im) + dot(exit_im, table_re)
    full_re = dot(table_re, half_re) - dot(table_im, half_im)
    full_im = dot(table_re, half_im) + dot(table_im, half_re)
    out_ref[...] = full_re * full_re + full_im * full_im

    for copy in finals:
        copy.wait_send()

    def sent(r):
        loop(1, SOURCES, lambda d: raw_copy(d, r).wait_send())
        loop(1, ny, lambda d: y_copy(d, r).wait_send())
        loop(1, nz, lambda d: z_copy(d, r).wait_send())
        e_each(r, lambda copy: copy.wait_send())

    loop(0, STRIPS, sent)


def probes(ny, nzh, smatrix, weights, tiles, own_mask, cut_mask, dft):
    nz = nzh * TILES
    each = nz * 4 + nzh * 4
    vmem = pl.BlockSpec(memory_space=pltpu.VMEM)
    half = jnp.bfloat16
    return pl.pallas_call(
        functools.partial(probe_kernel, ny, nzh),
        out_shape=jax.ShapeDtypeStruct((CROP, CROP), jnp.float32),
        in_specs=[pl.BlockSpec(memory_space=pl.ANY), vmem, vmem, vmem, vmem, vmem],
        out_specs=vmem,
        scratch_shapes=[
            pltpu.VMEM((STRIPS, SOURCES, 8, STRIP, FIELD), half),
            pltpu.VMEM((PLANES, DEPTH * STRIP, CROP), jnp.float32),
            pltpu.VMEM((ny * each * STRIP, CROP), jnp.float32),
            pltpu.VMEM((STRIPS, ny, each, STRIP, CROP), half),
            pltpu.VMEM((STRIPS, ny, each, STRIP, CROP), half),
            pltpu.VMEM((STRIPS, each, STRIP, CROP), half),
            pltpu.VMEM((STRIPS, nz, 4, STRIP, CROP), half),
            pltpu.VMEM((nz, 4, STRIP, CROP), half),
            pltpu.VMEM((4, STRIP, CROP), jnp.float32),
            pltpu.VMEM((2, STRIPS, 2, STRIP, CROP), jnp.float32),
            pltpu.VMEM((2, STRIPS, 2, STRIP, CROP), jnp.float32),
            pltpu.VMEM((3, STRIPS, 2, STRIP, CROP), jnp.float32),
            pltpu.VMEM((2, SOURCES, STRIP, CROP), jnp.float32),
            pltpu.SemaphoreType.DMA((STRIPS,)),
            pltpu.SemaphoreType.DMA((STRIPS, SOURCES)),
            pltpu.SemaphoreType.DMA((STRIPS, SOURCES)),
            pltpu.SemaphoreType.DMA((STRIPS, ny)),
            pltpu.SemaphoreType.DMA((STRIPS, ny)),
            pltpu.SemaphoreType.DMA((STRIPS, nz)),
            pltpu.SemaphoreType.DMA((STRIPS, nz)),
            pltpu.SemaphoreType.DMA((STRIPS, nzh)),
            pltpu.SemaphoreType.DMA((nz,)),
            pltpu.SemaphoreType.DMA((3,)),
            pltpu.SemaphoreType.DMA((3,)),
        ],
        compiler_params=pltpu.CompilerParams(
            collective_id=0, has_side_effects=True, vmem_limit_bytes=48 * 2**20
        ),
    )(smatrix, weights, tiles, own_mask, cut_mask, dft)


def dft_table():
    places = np.arange(CROP)
    angle = two_pi * (places[:, None] * places[None, :] % CROP) / CROP
    return np.stack([np.cos(angle), -np.sin(angle)]).astype(np.float32) / np.float32(math.sqrt(CROP))


def per_strip(values, x, c):
    ny, nzh = values.shape[2:4]
    own = lax.dynamic_index_in_dim(values, x, 0, False)
    before = lax.dynamic_index_in_dim(values, (x + PLANES - 1) % PLANES, 0, False)
    s = STRIPS * c + jnp.arange(STRIPS)
    zl = jnp.arange(TILES)
    main = jnp.where((zl[None, :] <= s[:, None])[:, :, None, None, None], own[None], before[None])
    extra = lax.dynamic_slice_in_dim(before, STRIPS * c, STRIPS, 0)
    main = main.transpose(0, 2, 3, 1, 4).reshape(STRIPS, ny, nzh * TILES * 2)
    return jnp.concatenate([main, extra.reshape(STRIPS, ny, nzh * 2)], axis=2)


def local(smatrix, offset_y, offset_x, beam_qx, beam_qy, beam_amp, beam_phase):
    x, zl, c = (lax.axis_index(a) for a in ("x", "zl", "c"))
    y, zh = lax.axis_index("y"), lax.axis_index("zh")
    ny, nzh = lax.axis_size("y"), lax.axis_size("zh")
    beams = BEAMS_PER
    total = beam_qx.shape[0] * ny * nzh * 2

    params = jnp.stack([beam_qx.astype(jnp.float32), beam_qy.astype(jnp.float32), beam_amp, beam_phase])
    params = lax.dynamic_index_in_dim(params.reshape(4, PLANES, TILES, beams), zl, 2, False)
    params = lax.all_gather(params, "c", axis=2)
    params = jnp.broadcast_to(params[:, :, :, None, :], (4, PLANES, 2, 2, beams)).reshape(4, DEPTH)
    qx, qy = params[0].astype(jnp.int32), params[1].astype(jnp.int32)
    amp, phase = params[2] * (1.0 / math.sqrt(total)), params[3]
    part = jnp.arange(DEPTH) // beams % 2

    grid = (PLANES, TILES, ny, nzh, 2)
    first_y = per_strip(offset_y.reshape(grid), x, c)
    first_x = per_strip(offset_x.reshape(grid), x, c)
    turns = (first_x + CROP // 2)[..., None] * qx + (first_y + CROP // 2)[..., None] * qy
    quarter = (jnp.arange(2)[:, None] - part[None, :]) * (FIELD // 4)
    turns = (turns[..., None, :] + quarter) % FIELD
    weights = (amp * jnp.cos(phase - two_pi * turns.astype(jnp.float32) / FIELD)).astype(jnp.bfloat16)
    count = first_x.shape[1] * first_x.shape[2] * 2
    weights = weights.reshape(STRIPS, count, DEPTH)
    lanes = jnp.arange(CROP)
    tiles = (first_x[..., None] // CROP + (lanes < (first_x % CROP)[..., None])) % PLANES
    tiles = jnp.broadcast_to(tiles[..., None, :], (*first_x.shape, 2, CROP)).reshape(STRIPS, count, CROP)

    s = STRIPS * c + jnp.arange(STRIPS)
    first = (y * nzh + zh) * 2
    per_tile = ny * nzh * 2
    own_y = lax.dynamic_slice_in_dim(offset_y, (x * TILES + zl) * per_tile + first, 2) % STRIP
    before_x = (x + PLANES - 1) % PLANES
    before_y = lax.dynamic_slice_in_dim(offset_y, (before_x * TILES + zl) * per_tile + first, 2) % STRIP
    i = jnp.arange(STRIP)
    own_mask = s[None, :, None] * STRIP + i >= zl * STRIP + own_y[:, None, None]
    own_mask = jnp.broadcast_to(own_mask[..., None].astype(jnp.float32), (2, STRIPS, STRIP, CROP))
    cut_mask = i < before_y[:, None]
    cut_mask = jnp.broadcast_to(cut_mask[..., None].astype(jnp.float32), (2, STRIP, CROP))
    smatrix = smatrix.reshape(2 * beams, FIELD, FIELD)
    return probes(ny, nzh, smatrix, weights, tiles, own_mask, cut_mask, jnp.asarray(dft_table()))[None]


BEAMS_PER = 4


def solution(mesh):
    tile, beam = mesh.shape["tile"], mesh.shape["beam"]
    del tile
    shape = (PLANES, TILES, beam // 4 if beam >= 4 else 1, 2 if beam >= 4 else 1, 2)
    fine = Mesh(mesh.devices.reshape(shape), ("x", "zl", "y", "zh", "c"))
    group = ("y", "zh", "c")
    return jax.shard_map(
        local,
        mesh=fine,
        in_specs=(P(None, (*group, "x", "zl"), None, None), P(), P(), P(group), P(group), P(group), P(group)),
        out_specs=P(("x", "zl", *group), None, None),
        check_vma=False,
    )
```

time: 326 us -> 130 us (0.40)
  waiting for transfers between devices: 227 us -> 0 us
  Pallas kernels: 21.5 us -> 106 us
  starting transfers between devices: 30.7 us -> 0 us
  between operations: 14 us -> 0.23 us
  local copies, waits for them, and re-layouts: 22.2 us -> 9.36 us
  blocking collectives: 1.81 us -> 8.37 us
  matrix products: 4.28 us -> 0 us
    unnamed x3 -> x0, waiting for transfers between devices: 129 us -> none
    pallas_call x1, Pallas kernels: 21.5 us -> 106 us  [probes(): pl.pallas_call(functools.partial(probe_kernel, ny, nzh), out_shape=jax.Sh...]
    reduce_scatter x1 -> x0, waiting for transfers between devices: 56.4 us -> none  [local(): waves = lax.psum_scatter(waves, 'y', scatter_dimension=1)]
    all_to_all x1 -> x0, waiting for transfers between devices: 40.4 us -> none  [local(): strips = lax.all_to_all(split, ('x', 'c'), split_axis=2, concat_axis=0)]
    ppermute x3 -> x0, starting transfers between devices: 19.2 us -> none  [sent(): return lax.ppermute(value, ('x', 'c'), pairs)]
    all_to_all x1 -> x0, starting transfers between devices: 11.5 us -> none  [local(): strips = lax.all_to_all(split, ('x', 'c'), split_axis=2, concat_axis=0)]
    all_gather x1, blocking collectives: 1.81 us -> 8.37 us  [local(): params = lax.all_gather(params, 'c', axis=2)]
    reshape x1 -> x0, local copies, waits for them, and re-layouts: 5.49 us -> none  [local(): waves = waves.reshape(STRIPS, ny, each, STRIP, CROP)]
  transfers between devices with their start and end apart: 6 -> 0, of which waited for: 4 -> 0; matrix products, arithmetic and copies ran while one was open for 3% -> 0% of each run, Pallas kernels for 0% -> 0%
where the time goes in v2:
time: 130 us; the launch traced here: 128 us
  Pallas kernels  106 us (82%)
  local copies, waits for them, and re-layouts  9.36 us (7%)
  blocking collectives  8.37 us (6%)
  other arithmetic  4.66 us (4%)
    pallas_call x1, Pallas kernels, probes(): pl.pallas_call(functools.partial(probe_kernel, ny, nzh), out_shape=jax.Sh...  106 us
    all_gather x1, blocking collectives, local(): params = lax.all_gather(params, 'c', axis=2)  8.37 us
    unnamed x7, local copies, waits for them, and re-layouts  2.84 us

profile of v2, /device:TPU:1, one launch (start us, length us, event | category | flops | bytes accessed | tf_op | source)
XLA Modules:
  0.0 128.5 jit_solution(811441317784006381)
XLA Ops:
  0.0 0.8 stack.18
  0.8 0.8 stack.17
  1.6 0.7 convert_element_type.66
  2.2 0.1 stack.16
  2.3 0.7 convert_element_type.65
  3.0 0.1 stack.15
  3.1 8.4 %all_gather.4 = f32[4,4,2,4]{3,1,0,2:T(4,128)S(1)} all-gather(f32[4,4,1,4]{3,1,0,2:T(4,128)S(1)} %bitcast.43), channel_id=1, replica_groups=mesh['x'=4,'zl'=8,'y'=4,'zh'=2,'c'=2] {'c'}, dimensions={2}, use_global_device_ids=true | all-gather | bytes 768 | tf_op jit(solution)/shard_map/all_gather | solution.py:359
  11.6 0.9 reshape.375
  12.6 0.9 reshape.374
  13.5 0.1 copy.57
  13.6 0.1 copy.58
  13.7 0.1 copy.45
  13.9 0.1 copy.46
  14.1 0.1 copy.42
  14.2 0.1 copy.43
  14.5 0.1 broadcast_in_dim.131
  14.7 0.1 copy.54
  14.8 0.1 copy.55
  15.0 0.1 copy.51
  15.1 0.1 copy.52
  15.4 0.1 convert_element_type.69
  15.5 0.1 copy.48
  15.6 0.1 copy.49
  15.7 0.1 add_select_fusion.3
  15.8 0.2 multiply_add_fusion
  16.1 0.2 add.224
  16.6 2.3 %fusion.6.weight_ref = bf16[4,288,64]{2,1,0:T(8,128)(2,1)S(1)} fusion(s32[4,288,64]{2,1,0:T(8,128)S(1)} %bitcast.37, s32[288,64]{1,0:T(8,128)S(1)} %bitcast.38, f32[64]{0:T(128)S(1)} %broadcast_in_dim.129, f32[64]{0:T(128)S(1)} %mul.112), kind=kLoop, calls=%fused_computation.9 | loop fusion | flops 1253376 | bytes 516608 | tf_op jit(solution)/shard_map/convert_element_type | solution.py:371
  18.8 0.2 add_select_fusion.1
  19.1 0.2 broadcast_in_dim.151
  19.8 2.2 %copy-done = bf16[2,4,512,512]{3,2,1,0:T(8,128)(2,1)S(1)} copy-done((bf16[2,4,512,512]{3,2,1,0:T(8,128)(2,1)S(1)}, bf16[2,4,512,512]{3,2,1,0:T(8,128)(2,1)}, u32[]{:S(2)}) %copy-start) | copy-done | bytes 4194328
  22.0 105.8 %shard_map.82 = f32[128,128]{1,0:T(8,128)S(1)} custom-call(bf16[8,512,512]{2,1,0:T(8,128)(2,1)S(1)} %bitcast.34, bf16[4,288,64]{2,1,0:T(8,128)(2,1)S(1)} %fusion.6.weight_ref, s32[4,288,128]{2,1,0:T(8,128)S(1)} %bitcast.35, f32[2,4,16,128]{3,2,1,0:T(8,128)S(1)} %broadcast_in_dim.152.own_mask, f32[2,16,128]{2,1,0:T(8,128)S(1)} %broadcast_in_dim.153.cut_mask, ...), custom_call_target="tpu_custom_call" | custom-call | tf_op jit(solution)/shard_map/pallas_call | solution.py:295
  127.8 0.6 copy.65
  (36 shorter events, 1.4 us)
Async XLA Ops:
  0.0 19.8 %copy-start.1 = (f32[2,128,128]{2,1,0:T(8,128)S(1)}, f32[2,128,128]{2,1,0:T(8,128)}, u32[]{:S(2)}) copy-start(f32[2,128,128]{2,1,0:T(8,128)} %constant.211.clone.dft) | copy-start | bytes 393220
  0.0 19.4 %copy-start.2 = (s32[512]{0:T(512)S(1)}, s32[512]{0:T(512)}, u32[]{:S(2)}) copy-start(s32[512]{0:T(512)} %param.9) | copy-start | bytes 6148
  19.8 2.2 %copy-start = (bf16[2,4,512,512]{3,2,1,0:T(8,128)(2,1)S(1)}, bf16[2,4,512,512]{3,2,1,0:T(8,128)(2,1)}, u32[]{:S(2)}) copy-start(bf16[2,4,512,512]{3,2,1,0:T(8,128)(2,1)} %param.8) | copy-start | bytes 12582916

commit v3 on v1

v3 whole, which is shorter than its diff:
```python
import functools
import math

import jax
import jax.numpy as jnp
import numpy as np
from jax import lax
from jax.experimental import pallas as pl
from jax.experimental.pallas import tpu as pltpu
from jax.sharding import Mesh
from jax.sharding import PartitionSpec as P

CROP = 128
STRIP = 16
FIELD = 512
PLANES = 4
TILES = 8
STRIPS = 4
SOURCES = 8
QUAD = 4
BEAMS_PER = 4
UNROLL = 4
DEPTH = 64

two_pi = 2.0 * math.pi


def remote(source, target, send_sem, recv_sem, device):
    return pltpu.make_async_remote_copy(
        src_ref=source,
        dst_ref=target,
        send_sem=send_sem,
        recv_sem=recv_sem,
        device_id=device,
        device_id_type=pl.DeviceIdType.MESH,
    )


def loop(start, stop, body):
    def step(i, carry):
        body(i)
        return carry

    lax.fori_loop(start, stop, step, 0)


def dft_table():
    places = np.arange(CROP)
    angle = two_pi * (places[:, None] * places[None, :] % CROP) / CROP
    return np.stack([np.cos(angle), -np.sin(angle)]).astype(np.float32) / np.float32(math.sqrt(CROP))


def probe_kernel(
    ny,
    nzh,
    smatrix,
    offset_y_ref,
    offset_x_ref,
    beam_qx_ref,
    beam_qy_ref,
    beam_amp_ref,
    beam_phase_ref,
    dft_ref,
    out_ref,
    offset_y,
    offset_x,
    beam_qx,
    beam_qy,
    beam_amp,
    beam_phase,
    raw,
    wide,
    rows,
    waves,
    ywave,
    relay,
    main1,
    extra1,
    zmain1,
    zextra1,
    main2,
    extra2,
    zmain2,
    zextra2,
    own_part,
    low_part,
    last,
    full,
    params,
    weight_own,
    weight_low,
    weight,
    tile_own,
    tile_low,
    tile,
    dft,
    local_sem,
    small_sem,
    a_send,
    a_recv,
    y_send,
    y_recv,
    z_send,
    z_recv,
    e_send,
    e_recv,
    f_send,
    f_recv,
    p_send,
    p_recv,
):
    x, zl, y, zh, c = (lax.axis_index(a) for a in ("x", "zl", "y", "zh", "c"))
    pair = nzh * 2
    per_tile = ny * pair
    per_plane = TILES * per_tile
    count = per_plane + per_tile
    each = (TILES + 1) * pair
    nq = nzh * 2
    half = zl // QUAD
    q, p = zh * 2 + half, lax.rem(zl, QUAD)
    me = x * 2 + c
    before_x = lax.rem(x + PLANES - 1, PLANES)
    other = 1 - c

    def peer(d):
        k = lax.rem(me + d, SOURCES)
        return k, {"x": k // 2, "c": lax.rem(k, 2)}

    def ypeer(d):
        k = lax.rem(y + d, ny)
        return k, {"y": k}

    def ppeer(d):
        k = lax.rem(p + d, QUAD)
        return k, {"zl": half * QUAD + k}

    def qpeer(d):
        k = lax.rem(q + d, nq)
        return k, {"zh": k // 2, "zl": lax.rem(k, 2) * QUAD + p}

    def greet(peers, number):
        def one(d):
            pl.semaphore_signal(
                pltpu.get_barrier_semaphore(), inc=1, device_id=peers(d)[1], device_id_type=pl.DeviceIdType.MESH
            )

        loop(1, number, one)

    beam_copies = [
        pltpu.make_async_copy(source, target, small_sem.at[j])
        for j, (source, target) in enumerate(
            (
                (beam_qx_ref, beam_qx),
                (beam_qy_ref, beam_qy),
                (beam_amp_ref, beam_amp),
                (beam_phase_ref, beam_phase),
            )
        )
    ]
    offset_copies = [
        pltpu.make_async_copy(offset_y_ref, offset_y, small_sem.at[4]),
        pltpu.make_async_copy(offset_x_ref, offset_x, small_sem.at[5]),
    ]
    dft_copy = pltpu.make_async_copy(dft_ref, dft, small_sem.at[6])
    for copy in (*beam_copies, *offset_copies, dft_copy):
        copy.start()
    greet(peer, SOURCES)
    for d in (1, ny - 1) if ny > 1 else ():
        pl.semaphore_signal(
            pltpu.get_barrier_semaphore(), inc=1, device_id=ypeer(d)[1], device_id_type=pl.DeviceIdType.MESH
        )
    greet(ppeer, QUAD)
    greet(qpeer, nq)
    pl.semaphore_wait(pltpu.get_barrier_semaphore(), SOURCES + min(ny - 1, 2) + QUAD + nq - 3)

    def part_rows(k, r):
        at = pl.ds(pl.multiple_of(k * (STRIPS * STRIP) + r * STRIP, STRIP), STRIP)
        return smatrix.at[:, :, at, :]

    def raw_copy(d, r):
        k, device = peer(d)
        return remote(part_rows(k, r), raw.at[r, me], a_send.at[r, k], a_recv.at[r, me], device)

    def raw_own(r):
        return pltpu.make_async_copy(part_rows(me, r), raw.at[r, me], local_sem.at[r])

    def raw_start(r):
        loop(1, SOURCES, lambda d: raw_copy(d, r).start())
        raw_own(r).start()

    for copy in beam_copies:
        copy.wait()
    params[0] = jnp.zeros((8, 128), jnp.float32)
    params[0, 0:1, :] = beam_qx[...].astype(jnp.float32).reshape(1, 128)
    params[0, 1:2, :] = beam_qy[...].astype(jnp.float32).reshape(1, 128)
    params[0, 2:3, :] = beam_amp[...].reshape(1, 128)
    params[0, 3:4, :] = beam_phase[...].reshape(1, 128)
    param_copy = remote(params.at[0], params.at[1], p_send, p_recv, {"c": other})
    param_copy.start()
    loop(0, STRIPS, raw_start)
    for copy in offset_copies:
        copy.wait()

    term = lax.broadcasted_iota(jnp.int32, (DEPTH, 128), 0)
    lane = lax.broadcasted_iota(jnp.int32, (DEPTH, 128), 1)
    hot = lane == ((term // 16) * TILES + zl) * BEAMS_PER + term % BEAMS_PER
    part = term[:, :1] // BEAMS_PER % 2
    param_copy.wait_recv()

    def column(j):
        mine, theirs = params[0, j : j + 1, :], params[1, j : j + 1, :]
        both = jnp.where(term // 8 % 2 == c, mine, theirs)
        return jnp.sum(jnp.where(hot, both, 0.0), axis=1, keepdims=True)

    qx, qy = column(0).astype(jnp.int32), column(1).astype(jnp.int32)
    amp = column(2) * (1.0 / math.sqrt(ny * nzh * 2 * 128))
    phase = column(3)

    def plane_values(ref, plane):
        return ref[pl.ds(pl.multiple_of(plane * per_plane, per_plane), per_plane)].reshape(1, per_plane)

    for plane, to_weight, to_tile in ((x, weight_own, tile_own), (before_x, weight_low, tile_low)):
        first_y, first_x = plane_values(offset_y, plane), plane_values(offset_x, plane)
        turns = (first_x + CROP // 2) * qx + (first_y + CROP // 2) * qy
        for k in range(2):
            turned = (turns + (k - part) * (FIELD // 4)) & (FIELD - 1)
            value = amp * jnp.cos(phase - turned.astype(jnp.float32) * (two_pi / FIELD))
            to_weight[k] = value.T
        column_lane = lax.broadcasted_iota(jnp.int32, (CROP, per_plane), 0)
        place = (first_x // CROP + jnp.where(column_lane < (first_x & (CROP - 1)), 1, 0)) & (PLANES - 1)
        to_tile[...] = place.T

    def raw_wait(d, r):
        k, device = peer(d)
        remote(raw.at[r, k], raw.at[r, k], a_send.at[r, k], a_recv.at[r, k], device).wait_recv()

    cut = each // 2
    far = ypeer(2)[0]

    def y_near(d, r, k):
        t, device = ypeer(1 if d == 0 else ny - 1)
        at = pl.ds(cut, cut) if d == 0 else pl.ds(0, cut)
        return remote(
            waves.at[r, k, t, at], ywave.at[r, k, d, at], y_send.at[r, k, d], y_recv.at[r, k, d], device
        )

    def y_far(d, r, k):
        device = ypeer(1 if d == 0 else ny - 1)[1]
        at = pl.ds(0, cut) if d == 0 else pl.ds(cut, cut)
        return remote(
            waves.at[r, k, far, at], relay.at[r, k, d], y_send.at[r, k, 2 + d], y_recv.at[r, k, 2 + d], device
        )

    def y_last(d, r, k):
        t, device = ypeer(1 if d == 0 else ny - 1)
        at = pl.ds(0, cut) if d == 0 else pl.ds(cut, cut)
        return remote(
            waves.at[r, k, t, at], ywave.at[r, k, d, at], y_send.at[r, k, 4 + d], y_recv.at[r, k, 4 + d], device
        )

    def y_start(r, k):
        if ny > 1:
            for make in (y_far, y_near):
                for d in range(2):
                    make(d, r, k).start()

    def y_relay(r, k):
        if ny > 1:
            for d in range(2):
                y_far(d, r, k).wait_recv()
                t = ypeer(1 if d == 0 else ny - 1)[0]
                at = pl.ds(0, cut) if d == 0 else pl.ds(cut, cut)
                value = waves[r, k, t, at].astype(jnp.float32) + relay[r, k, d].astype(jnp.float32)
                waves[r, k, t, at] = value.astype(jnp.bfloat16)
                y_last(d, r, k).start()

    def y_done(r, k):
        if ny > 1:
            for make in (y_far, y_near, y_last):
                for d in range(2):
                    make(d, r, k).wait_send()

    def z1_copy(d, r, k):
        t, device = ppeer(d)
        return remote(main1.at[r, k, :, t], zmain1.at[r, k, p], z_send.at[0, r, k, t], z_recv.at[0, r, k, p], device)

    def z1_wait(d, r, k):
        t, device = ppeer(d)
        remote(
            zmain1.at[r, k, t], zmain1.at[r, k, t], z_send.at[0, r, k, t], z_recv.at[0, r, k, t], device
        ).wait_recv()

    def e1_copy(r, k):
        return remote(
            extra1.at[r, k], zextra1.at[k, p], e_send.at[0, r, k], e_recv.at[0, k, p], {"zl": half * QUAD + r}
        )

    def e1_wait(d, k):
        t, device = ppeer(d)
        remote(zextra1.at[k, t], zextra1.at[k, t], e_send.at[0, 0, k], e_recv.at[0, k, t], device).wait_recv()

    def z2_copy(d, r, k):
        t, device = qpeer(d)
        return remote(
            main2.at[r, k, lax.rem(t, 2), pl.ds(t // 2 * 2, 2)],
            zmain2.at[r, k, q],
            z_send.at[1, r, k, t],
            z_recv.at[1, r, k, q],
            device,
        )

    def z2_wait(d, r, k):
        t, device = qpeer(d)
        remote(
            zmain2.at[r, k, t], zmain2.at[r, k, t], z_send.at[1, r, k, t], z_recv.at[1, r, k, t], device
        ).wait_recv()

    def e2_copy(h, k):
        return remote(
            extra2.at[k, pl.ds(h * 2, 2)],
            zextra2.at[k, q],
            e_send.at[1, h, k],
            e_recv.at[1, k, q],
            {"zh": h, "zl": c * QUAD + p},
        )

    def e2_each(k, act):
        def one(h):
            @pl.when(h * 2 + c != q)
            def _():
                act(e2_copy(h, k))

        loop(0, nzh, one)

    def e2_wait(d, k):
        t, device = qpeer(d)
        remote(zextra2.at[k, t], zextra2.at[k, t], e_send.at[1, 0, k], e_recv.at[1, k, t], device).wait_recv()

    def mixing(r):
        s = c * STRIPS + r
        tile_of = lax.broadcasted_iota(jnp.int32, (per_plane, DEPTH), 0) // per_tile
        place_of = lax.broadcasted_iota(jnp.int32, (per_plane, CROP), 0) // per_tile
        crossing = pl.ds(pl.multiple_of(s * per_tile, per_tile), per_tile)
        for k in range(2):
            start = k * count
            main = jnp.where(tile_of <= s, weight_own[k], weight_low[k])
            weight[start : start + per_plane] = main.astype(jnp.bfloat16)
            weight[start + per_plane : start + count] = weight_low[k, crossing].astype(jnp.bfloat16)
        tile[:per_plane] = jnp.where(place_of <= s, tile_own[...], tile_low[...])
        tile[per_plane:] = tile_low[crossing]
        raw_own(r).wait()
        loop(1, SOURCES, lambda d: raw_wait(d, r))

        def widen(b):
            for k in range(PLANES):
                block = raw[r, b, :, :, :, k * CROP : (k + 1) * CROP].astype(jnp.float32)
                wide[k, pl.ds(pl.multiple_of(b * 128, 128), 128), :] = block.reshape(128, CROP)

        loop(0, SOURCES, widen)

        def one_row(i):
            field_row = jnp.concatenate(
                [wide[k, pl.ds(i, DEPTH, stride=STRIP), :].astype(jnp.bfloat16) for k in range(PLANES)], axis=1
            )
            product = jnp.dot(weight[...], field_row, preferred_element_type=jnp.float32)
            place = tile[...]
            for k in range(2):
                here = product[k * count : (k + 1) * count]
                picked = jnp.where(
                    place < 2,
                    jnp.where(place == 0, here[:, :128], here[:, 128:256]),
                    jnp.where(place == 2, here[:, 256:384], here[:, 384:]),
                )
                rows[k, pl.ds(i, count, stride=STRIP), :] = picked

        def some_rows(i):
            for j in range(UNROLL):
                one_row(i * UNROLL + j)

        loop(0, STRIP // UNROLL, some_rows)

        for k in range(2):

            def narrow(j):
                size = pair * STRIP
                block = rows[k, pl.ds(pl.multiple_of(j * size, STRIP), size), :].astype(jnp.bfloat16)
                waves[r, k, lax.rem(j, ny), pl.ds(j // ny * pair, pair)] = block.reshape(pair, STRIP, CROP)

            loop(0, (TILES + 1) * ny, narrow)
            y_start(r, k)

    def y_sum(r, k):
        if ny > 1:
            for d in range(2):
                y_near(d, r, k).wait_recv()
                y_last(d, r, k).wait_recv()

        def total(g):
            at = pl.ds(g * pair, pair)
            value = waves[r, k, y, at].astype(jnp.float32)
            for d in range(min(ny - 1, 2)):
                value += ywave[r, k, d, at].astype(jnp.float32)
            return value.astype(jnp.bfloat16)

        def block(g):
            main1[r, k, g // QUAD, lax.rem(g, QUAD)] = total(g)

        loop(0, TILES, block)
        extra1[r, k] = total(TILES)
        loop(1, QUAD, lambda d: z1_copy(d, r, k).start())

        @pl.when(p != r)
        def _():
            e1_copy(r, k).start()

    def z1_sum(r, k):
        loop(1, QUAD, lambda d: z1_wait(d, r, k))
        for a in range(2):
            value = main1[r, k, a, p].astype(jnp.float32)
            for d in range(1, QUAD):
                value += zmain1[r, k, ppeer(d)[0], a].astype(jnp.float32)
            main2[r, k, a] = value.astype(jnp.bfloat16)
        loop(1, nq, lambda d: z2_copy(d, r, k).start())

        @pl.when(p == r)
        def _():
            loop(1, QUAD, lambda d: e1_wait(d, k))
            value = extra1[r, k].astype(jnp.float32)
            for d in range(1, QUAD):
                value += zextra1[k, ppeer(d)[0]].astype(jnp.float32)
            extra2[k] = value.astype(jnp.bfloat16)
            e2_each(k, lambda copy: copy.start())

    def stage(r):
        @pl.when(r > 0)
        def _():
            y_sum(r - 1, 0)

        @pl.when(r > 1)
        def _():
            z1_sum(r - 2, 1)

        mixing(r)

        @pl.when(r > 0)
        def _():
            y_sum(r - 1, 1)
            z1_sum(r - 1, 0)

        y_relay(r, 0)
        y_relay(r, 1)

    loop(0, STRIPS, stage)
    spot = lax.broadcasted_iota(jnp.int32, (1, per_plane), 1)
    row = lax.broadcasted_iota(jnp.int32, (STRIP, CROP), 0)
    mine = zl * per_tile + (y * nzh + zh) * 2

    def first_row(plane, k):
        picked = jnp.where(spot == mine + k, plane_values(offset_y, plane) & (STRIP - 1), 0)
        return jnp.sum(picked.astype(jnp.float32), axis=1, keepdims=True).astype(jnp.int32)

    own_rows = [row >= first_row(x, k) for k in range(2)]
    cut_rows = [row < first_row(before_x, k) for k in range(2)]

    def final_copies(r):
        return [
            remote(own_part.at[other, r], last.at[0, r], f_send.at[0, r], f_recv.at[0, r], {"c": other}),
            remote(low_part.at[c, r], last.at[1, r], f_send.at[1, r], f_recv.at[1, r], {"x": before_x}),
            remote(low_part.at[other, r], last.at[2, r], f_send.at[2, r], f_recv.at[2, r], {"x": before_x, "c": other}),
        ]

    def closing(r):
        s = c * STRIPS + r
        own = jnp.where(s > zl, 1.0, 0.0)
        low = jnp.where(s < zl, 1.0, 0.0)
        edge = jnp.where(s == zl, 1.0, 0.0)
        for k in range(2):
            loop(1, nq, lambda d: z2_wait(d, r, k))
            value = main2[r, k, half, pl.ds(zh * 2, 2)].astype(jnp.float32)
            for d in range(1, nq):
                value += zmain2[r, k, qpeer(d)[0]].astype(jnp.float32)
            for j in range(2):
                own_part[j, r, k] = value[j] * (own + jnp.where(own_rows[j], edge, 0.0))
                low_part[j, r, k] = value[j] * low

        @pl.when(s == zl)
        def _():
            for k in range(2):
                loop(1, nq, lambda d: e2_wait(d, k))
                value = extra2[k, pl.ds(zh * 2, 2)].astype(jnp.float32)
                for d in range(1, nq):
                    value += zextra2[k, qpeer(d)[0]].astype(jnp.float32)
                for j in range(2):
                    low_part[j, r, k] = jnp.where(cut_rows[j], value[j], 0.0)

        for copy in final_copies(r):
            copy.start()

    def dot(a, b):
        return jnp.dot(a, b, precision=lax.Precision.HIGHEST, preferred_element_type=jnp.float32)

    def finish(r):
        for copy in final_copies(r):
            copy.wait_recv()
        exits = [own_part[c, r, k] + last[1, r, k] for k in range(2)]
        exits += [last[0, r, k] + last[2, r, k] for k in range(2)]
        lines = dot(jnp.concatenate(exits, axis=0), jnp.concatenate([dft[0], dft[1]], axis=1))
        for core, k in ((c, 0), (other, 2)):
            real, imag = lines[k * STRIP : (k + 1) * STRIP], lines[(k + 1) * STRIP : (k + 2) * STRIP]
            full[core * STRIPS + r, :, :CROP] = real[:, :CROP] - imag[:, CROP:]
            full[core * STRIPS + r, :, CROP:] = real[:, CROP:] + imag[:, :CROP]

    z1_sum(STRIPS - 2, 1)
    y_sum(STRIPS - 1, 0)
    dft_copy.wait()
    loop(0, STRIPS - 2, closing)
    y_sum(STRIPS - 1, 1)
    closing(STRIPS - 2)
    z1_sum(STRIPS - 1, 0)
    z1_sum(STRIPS - 1, 1)

    def sent(r):
        loop(1, SOURCES, lambda d: raw_copy(d, r).wait_send())
        for k in range(2):
            y_done(r, k)
            loop(1, QUAD, lambda d: z1_copy(d, r, k).wait_send())
            loop(1, nq, lambda d: z2_copy(d, r, k).wait_send())

            @pl.when(p != r)
            def _():
                e1_copy(r, k).wait_send()

            @pl.when(p == r)
            def _():
                e2_each(k, lambda copy: copy.wait_send())

    loop(0, STRIPS - 1, finish)
    closing(STRIPS - 1)
    loop(0, STRIPS, sent)
    param_copy.wait_send()
    finish(STRIPS - 1)
    spectrum = dot(jnp.concatenate([dft[0], dft[1]], axis=0), full[...].reshape(CROP, 2 * CROP))
    full_re = spectrum[:CROP, :CROP] - spectrum[CROP:, CROP:]
    full_im = spectrum[:CROP, CROP:] + spectrum[CROP:, :CROP]
    out_ref[0] = full_re * full_re + full_im * full_im

    def final_sent(r):
        for copy in final_copies(r):
            copy.wait_send()

    loop(0, STRIPS, final_sent)


def local(smatrix, offset_y, offset_x, beam_qx, beam_qy, beam_amp, beam_phase):
    ny, nzh = lax.axis_size("y"), lax.axis_size("zh")
    pair = nzh * 2
    per_plane = TILES * ny * pair
    count = per_plane + ny * pair
    each = (TILES + 1) * pair
    nq = nzh * 2
    vmem = pl.BlockSpec(memory_space=pltpu.VMEM)
    hbm = pl.BlockSpec(memory_space=pltpu.HBM)
    bf16, f32 = jnp.bfloat16, jnp.float32

    def blocks(kind, *lead):
        return pltpu.VMEM((*lead, STRIP, CROP), kind)

    dma = pltpu.SemaphoreType.DMA
    return pl.pallas_call(
        functools.partial(probe_kernel, ny, nzh),
        out_shape=jax.ShapeDtypeStruct((1, CROP, CROP), f32),
        in_specs=[hbm] * 8,
        out_specs=vmem,
        scratch_shapes=[
            pltpu.VMEM(offset_y.shape, jnp.int32),
            pltpu.VMEM(offset_x.shape, jnp.int32),
            pltpu.VMEM(beam_qx.shape, jnp.int32),
            pltpu.VMEM(beam_qy.shape, jnp.int32),
            pltpu.VMEM(beam_amp.shape, f32),
            pltpu.VMEM(beam_phase.shape, f32),
            pltpu.VMEM((STRIPS, SOURCES, 2, BEAMS_PER, STRIP, FIELD), bf16),
            pltpu.VMEM((PLANES, DEPTH * STRIP, CROP), f32),
            pltpu.VMEM((2, count * STRIP, CROP), f32),
            blocks(bf16, STRIPS, 2, ny, each),
            blocks(bf16, STRIPS, 2, 2, each),
            blocks(bf16, STRIPS, 2, 2, each // 2),
            blocks(bf16, STRIPS, 2, 2, QUAD, pair),
            blocks(bf16, STRIPS, 2, pair),
            blocks(bf16, STRIPS, 2, QUAD, 2, pair),
            blocks(bf16, 2, QUAD, pair),
            blocks(bf16, STRIPS, 2, 2, pair),
            blocks(bf16, 2, pair),
            blocks(bf16, STRIPS, 2, nq, 2),
            blocks(bf16, 2, nq, 2),
            blocks(f32, 2, STRIPS, 2),
            blocks(f32, 2, STRIPS, 2),
            blocks(f32, 3, STRIPS, 2),
            pltpu.VMEM((SOURCES, STRIP, 2 * CROP), f32),
            pltpu.VMEM((2, 8, 128), f32),
            pltpu.VMEM((2, per_plane, DEPTH), f32),
            pltpu.VMEM((2, per_plane, DEPTH), f32),
            pltpu.VMEM((2 * count, DEPTH), bf16),
            pltpu.VMEM((per_plane, CROP), jnp.int32),
            pltpu.VMEM((per_plane, CROP), jnp.int32),
            pltpu.VMEM((count, CROP), jnp.int32),
            pltpu.VMEM((2, CROP, CROP), f32),
            dma((STRIPS,)),
            dma((7,)),
            dma((STRIPS, SOURCES)),
            dma((STRIPS, SOURCES)),
            dma((STRIPS, 2, 6)),
            dma((STRIPS, 2, 6)),
            dma((2, STRIPS, 2, QUAD)),
            dma((2, STRIPS, 2, QUAD)),
            dma((2, STRIPS, 2)),
            dma((2, 2, QUAD)),
            dma((3, STRIPS)),
            dma((3, STRIPS)),
            dma,
            dma,
        ],
        compiler_params=pltpu.CompilerParams(
            collective_id=0, has_side_effects=True, vmem_limit_bytes=60 * 2**20
        ),
    )(smatrix, offset_y, offset_x, beam_qx, beam_qy, beam_amp, beam_phase, jnp.asarray(dft_table()))


def solution(mesh):
    tile, beam = mesh.shape["tile"], mesh.shape["beam"]
    del tile
    shape = (PLANES, TILES, beam // 4 if beam >= 4 else 1, 2 if beam >= 4 else 1, 2)
    fine = Mesh(mesh.devices.reshape(shape), ("x", "zl", "y", "zh", "c"))
    group = ("y", "zh", "c")
    return jax.shard_map(
        local,
        mesh=fine,
        in_specs=(P(None, (*group, "x", "zl"), None, None), P(), P(), P(group), P(group), P(group), P(group)),
        out_specs=P(("x", "zl", *group), None, None),
        check_vma=False,
    )
```

time: 326 us -> 103 us (0.32)
  waiting for transfers between devices: 227 us -> 0 us
  Pallas kernels: 21.5 us -> 102 us
  starting transfers between devices: 30.7 us -> 0 us
  local copies, waits for them, and re-layouts: 22.2 us -> 1.47 us
  between operations: 14 us -> 0.01 us
  other arithmetic: 4.78 us -> 0 us
  matrix products: 4.28 us -> 0 us
    unnamed x3 -> x0, waiting for transfers between devices: 129 us -> none
    pallas_call x1, Pallas kernels: 21.5 us -> 102 us  [local(): pl.pallas_call(functools.partial(probe_kernel, ny, nzh), out_shape=jax.Sh...]
    reduce_scatter x1 -> x0, waiting for transfers between devices: 56.4 us -> none  [local(): waves = lax.psum_scatter(waves, 'y', scatter_dimension=1)]
    all_to_all x1 -> x0, waiting for transfers between devices: 40.4 us -> none  [local(): strips = lax.all_to_all(split, ('x', 'c'), split_axis=2, concat_axis=0)]
    ppermute x3 -> x0, starting transfers between devices: 19.2 us -> none  [sent(): return lax.ppermute(value, ('x', 'c'), pairs)]
    all_to_all x1 -> x0, starting transfers between devices: 11.5 us -> none  [local(): strips = lax.all_to_all(split, ('x', 'c'), split_axis=2, concat_axis=0)]
    reshape x3 -> x0, local copies, waits for them, and re-layouts: 5.93 us -> none  [the longest x1 5.49 us: local(): waves = waves.reshape(STRIPS, ny, each, STRIP, CROP)]
    another operation x5 -> x0, local copies, waits for them, and re-layouts: 5.21 us -> none  [the longest x1 4.83 us: local(): strips = lax.all_to_all(split, ('x', 'c'), split_axis=2, concat_axis=0)]
  transfers between devices with their start and end apart: 6 -> 0, of which waited for: 4 -> 0; matrix products, arithmetic and copies ran while one was open for 3% -> 0% of each run, Pallas kernels for 0% -> 0%
where the time goes in v3:
time: 103 us
  Pallas kernels  102 us (99%)
  local copies, waits for them, and re-layouts  1.47 us (1%)
    pallas_call x1, Pallas kernels, local(): pl.pallas_call(functools.partial(probe_kernel, ny, nzh), out_shape=jax.Sh...  102 us

profile of v3, /device:TPU:1, one launch (start us, length us, event | category | flops | bytes accessed | tf_op | source)
XLA Modules:
  0.0 103.1 jit_solution(7361512846794379171)
XLA Ops:
  0.0 101.7 %shard_map.82 = f32[1,128,128]{2,1,0:T(8,128)} custom-call(bf16[2,4,512,512]{3,2,1,0:T(8,128)(2,1)} %smatrix.1, s32[512]{0:T(512)} %offset_y_ref.1, s32[512]{0:T(512)} %offset_x_ref.1, s32[128]{0:T(128)} %beam_qx_ref.1, s32[128]{0:T(128)} %beam_qy_ref.1, f32[128]{0:T(128)} %beam_amp_ref.1, f32[128]{0:T(128)} %beam_phase_ref.1, ...), custom_call_target="tpu_custom_call" | custom-call | tf_op jit(solution)/shard_map/pallas_call | solution.py:569
  101.7 1.5 %copy.10 = f32[1,128,128]{2,1,0:T(8,128)} copy(f32[1,128,128]{2,1,0:T(8,128)} %shard_map.82) | data formatting | bytes 131072

commit v4 on v3

--- a/solution.py
+++ b/solution.py
@@ -19,7 +19,7 @@
 SOURCES = 8
 QUAD = 4
 BEAMS_PER = 4
-UNROLL = 4
+UNROLL = 8
 DEPTH = 64
 
 two_pi = 2.0 * math.pi
@@ -358,28 +358,26 @@
 
         loop(0, SOURCES, widen)
 
-        def one_row(i):
+        def one_row(i, k):
             field_row = jnp.concatenate(
-                [wide[k, pl.ds(i, DEPTH, stride=STRIP), :].astype(jnp.bfloat16) for k in range(PLANES)], axis=1
+                [wide[t, pl.ds(i, DEPTH, stride=STRIP), :].astype(jnp.bfloat16) for t in range(PLANES)], axis=1
             )
-            product = jnp.dot(weight[...], field_row, preferred_element_type=jnp.float32)
+            here = jnp.dot(weight[k * count : (k + 1) * count], field_row, preferred_element_type=jnp.float32)
             place = tile[...]
-            for k in range(2):
-                here = product[k * count : (k + 1) * count]
-                picked = jnp.where(
-                    place < 2,
-                    jnp.where(place == 0, here[:, :128], here[:, 128:256]),
-                    jnp.where(place == 2, here[:, 256:384], here[:, 384:]),
-                )
-                rows[k, pl.ds(i, count, stride=STRIP), :] = picked
-
-        def some_rows(i):
-            for j in range(UNROLL):
-                one_row(i * UNROLL + j)
-
-        loop(0, STRIP // UNROLL, some_rows)
+            picked = jnp.where(
+                place < 2,
+                jnp.where(place == 0, here[:, :128], here[:, 128:256]),
+                jnp.where(place == 2, here[:, 256:384], here[:, 384:]),
+            )
+            rows[k, pl.ds(i, count, stride=STRIP), :] = picked
 
         for k in range(2):
+
+            def some_rows(i):
+                for j in range(UNROLL):
+                    one_row(i * UNROLL + j, k)
+
+            loop(0, STRIP // UNROLL, some_rows)
 
             def narrow(j):
                 size = pair * STRIP
@@ -441,13 +439,13 @@
             z1_sum(r - 2, 1)
 
         mixing(r)
+        y_relay(r, 0)
 
         @pl.when(r > 0)
         def _():
             y_sum(r - 1, 1)
             z1_sum(r - 1, 0)
 
-        y_relay(r, 0)
         y_relay(r, 1)
 
     loop(0, STRIPS, stage)
@@ -535,9 +533,9 @@
                 e2_each(k, lambda copy: copy.wait_send())
 
     loop(0, STRIPS - 1, finish)
-    closing(STRIPS - 1)
     loop(0, STRIPS, sent)
     param_copy.wait_send()
+    closing(STRIPS - 1)
     finish(STRIPS - 1)
     spectrum = dot(jnp.concatenate([dft[0], dft[1]], axis=0), full[...].reshape(CROP, 2 * CROP))
     full_re = spectrum[:CROP, :CROP] - spectrum[CROP:, CROP:]

time: 103 us -> 102 us (level)
  Pallas kernels: 102 us -> 100 us
    pallas_call x1, Pallas kernels: 102 us -> 100 us  [local(): pl.pallas_call(functools.partial(probe_kernel, ny, nzh), out_shape=jax.Sh...]
where the time goes in v4:
time: 102 us; the launch traced here: 101 us
  Pallas kernels  100 us (98%)
  local copies, waits for them, and re-layouts  1.47 us (1%)
    pallas_call x1, Pallas kernels, local(): pl.pallas_call(functools.partial(probe_kernel, ny, nzh), out_shape=jax.Sh...  100 us

profile of v4, /device:TPU:1, one launch (start us, length us, event | category | flops | bytes accessed | tf_op | source)
XLA Modules:
  0.0 101.5 jit_solution(16454152927611324261)
XLA Ops:
  0.0 100.0 %shard_map.82 = f32[1,128,128]{2,1,0:T(8,128)} custom-call(bf16[2,4,512,512]{3,2,1,0:T(8,128)(2,1)} %smatrix.1, s32[512]{0:T(512)} %offset_y_ref.1, s32[512]{0:T(512)} %offset_x_ref.1, s32[128]{0:T(128)} %beam_qx_ref.1, s32[128]{0:T(128)} %beam_qy_ref.1, f32[128]{0:T(128)} %beam_amp_ref.1, f32[128]{0:T(128)} %beam_phase_ref.1, ...), custom_call_target="tpu_custom_call" | custom-call | tf_op jit(solution)/shard_map/pallas_call | solution.py:567
  100.0 1.5 %copy.10 = f32[1,128,128]{2,1,0:T(8,128)} copy(f32[1,128,128]{2,1,0:T(8,128)} %shard_map.82) | data formatting | bytes 131072
